TPU v7x, 256 devices: a whole 4x4x8 slice. The times are simulated.
256 devices in a mesh: dp: 16 (over z, core), seq: 16 (over y, x).
Axes of the slice: x: 4, y: 4, z: 8, core: 2. Of those that a mesh axis runs over, the one named last changes fastest.
Arguments:
- queries: bfloat16 [16, 2048, 1024], P('dp', 'seq'), may hold values from -8 to 8
- key_vectors: bfloat16 [16, 2048, 1024], P('dp', 'seq'), may hold values from -8 to 8
- value_vectors: bfloat16 [16, 2048, 1024], P('dp', 'seq'), may hold values from -6 to 6
- out_grad: bfloat16 [16, 2048, 1024], P('dp', 'seq'), may hold values from -6 to 6
- proj_weight: bfloat16 [1024, 1024], P(None, 'seq'), may hold values from -0.1875 to 0.1875
- cluster_order: int32 [16, 2048], P('dp'), may hold values from 0 to 2047, as said below
- block_cols: int32 [16, 32, 16], P('dp'), may hold values from 0 to 31, as said below
- block_count: int32 [16, 32], P('dp'), may hold values from 5 to 16, as said below
Outputs:
- layer_out: bfloat16 [16, 2048, 1024], P('dp', 'seq')
- query_grad: bfloat16 [16, 2048, 1024], P('dp', 'seq')
- key_grad: bfloat16 [16, 2048, 1024], P('dp', 'seq')
- value_grad: bfloat16 [16, 2048, 1024], P('dp', 'seq')
- weight_grad: float32 [1024, 1024], P(None, 'seq')
Inputs may be any that keep to these rules, and one draw needn't show every extreme that they name: `cluster_order`: each graph's row is a permutation of the 2048 nodes. `block_cols`: the entries of one list are distinct and the list of row block r begins with r itself; entries at positions block_count or later are ignored. `block_count`: some row block of every graph has 16 live entries.
All inputs are finite; a program needn't handle non-finite values.
Results may differ from a plain program's by a relative error of at most 0.029.
Values may be sent and summed in bfloat16 or wider, within the bound.
A program may use at most 64 MiB of HBM per device.

v0:
```python
import jax
import jax.numpy as jnp
from jax import lax
from jax.sharding import PartitionSpec as P

HEADS = 16


def head_pass(
    query_rows, key_rows, value_rows, upstream_rows, col_blocks, block_counts, score_scale
):
    block_total = col_blocks.shape[0]
    list_len = col_blocks.shape[1]
    block_len = query_rows.shape[0] // block_total
    head_size = query_rows.shape[1]
    tile_width = block_len * head_size
    row_blocks = min(8, block_total)
    groups = block_total // row_blocks
    query_tiles = query_rows.reshape(groups, row_blocks, block_len, head_size)
    upstream_tiles = upstream_rows.reshape(groups, row_blocks, block_len, head_size)
    key_flat = key_rows.reshape(block_total, tile_width)
    value_flat = value_rows.reshape(block_total, tile_width)
    group_cols_all = col_blocks.reshape(groups, row_blocks, list_len)
    group_count_all = block_counts.reshape(groups, row_blocks)
    block_ids = jnp.arange(block_total, dtype=jnp.int32)

    def group_step(state, inputs):
        key_acc, value_acc = state
        query_tile, upstream_tile, group_cols, group_count = inputs
        selector = group_cols[:, :, None] == block_ids[None, None, :]
        listed = selector.astype(jnp.bfloat16)
        key_tiles = jnp.einsum(
            "rmn,nk->rmk", listed, key_flat, preferred_element_type=jnp.float32
        ).astype(jnp.bfloat16)
        value_tiles = jnp.einsum(
            "rmn,nk->rmk", listed, value_flat, preferred_element_type=jnp.float32
        ).astype(jnp.bfloat16)
        key_tiles = key_tiles.reshape(row_blocks, list_len, block_len, head_size)
        value_tiles = value_tiles.reshape(row_blocks, list_len, block_len, head_size)
        score = (
            jnp.einsum("rid,rmjd->rimj", query_tile, key_tiles, preferred_element_type=jnp.float32)
            * score_scale
        )
        live_mask = (jnp.arange(list_len)[None, :] < group_count[:, None])[:, None, :, None]
        masked = jnp.where(live_mask, score, -jnp.inf)
        row_max = jnp.max(masked, axis=(2, 3), keepdims=True)
        exp_terms = jnp.exp(masked - row_max)
        denominator = jnp.sum(exp_terms, axis=(2, 3), keepdims=True)
        softmax = exp_terms / denominator
        softmax_half = softmax.astype(jnp.bfloat16)
        output_tile = jnp.einsum(
            "rimj,rmjd->rid", softmax_half, value_tiles, preferred_element_type=jnp.float32
        ).astype(jnp.bfloat16)
        row_delta = jnp.sum(
            output_tile.astype(jnp.float32) * upstream_tile.astype(jnp.float32), axis=-1
        )[:, :, None, None]
        grad_softmax = jnp.einsum(
            "rid,rmjd->rimj", upstream_tile, value_tiles, preferred_element_type=jnp.float32
        )
        grad_score = (score_scale * softmax * (grad_softmax - row_delta)).astype(jnp.bfloat16)
        grad_query = jnp.einsum(
            "rimj,rmjd->rid", grad_score, key_tiles, preferred_element_type=jnp.float32
        ).astype(jnp.bfloat16)
        key_terms = jnp.einsum(
            "rimj,rid->rmjd", grad_score, query_tile, preferred_element_type=jnp.float32
        )
        value_terms = jnp.einsum(
            "rimj,rid->rmjd", softmax_half, upstream_tile, preferred_element_type=jnp.float32
        )
        listed_f = selector.astype(jnp.float32)
        key_acc = key_acc + jnp.einsum(
            "rmn,rmk->nk",
            listed_f,
            key_terms.reshape(row_blocks, list_len, tile_width),
            precision=lax.Precision.HIGHEST,
        )
        value_acc = value_acc + jnp.einsum(
            "rmn,rmk->nk",
            listed_f,
            value_terms.reshape(row_blocks, list_len, tile_width),
            precision=lax.Precision.HIGHEST,
        )
        return ((key_acc, value_acc), (output_tile, grad_query))

    start_state = (
        jnp.zeros((block_total, tile_width), jnp.float32),
        jnp.zeros((block_total, tile_width), jnp.float32),
    )
    (key_acc, value_acc), (outputs, grad_queries) = lax.scan(
        group_step, start_state, (query_tiles, upstream_tiles, group_cols_all, group_count_all)
    )
    return (
        outputs.reshape(-1, head_size),
        grad_queries.reshape(-1, head_size),
        key_acc.reshape(-1, head_size).astype(jnp.bfloat16),
        value_acc.reshape(-1, head_size).astype(jnp.bfloat16),
    )


def on_device(
    queries,
    key_vectors,
    value_vectors,
    out_grad,
    proj_weight,
    cluster_order,
    block_cols,
    block_count,
):
    seq_devices = lax.axis_size("seq")
    nodes_dev = queries.shape[1]
    feature_width = queries.shape[2]
    head_count = HEADS
    head_size = feature_width // head_count
    local_heads = head_count // seq_devices
    score_scale = head_size ** (-0.5)
    node_order = cluster_order[0]
    col_blocks = block_cols[0]
    block_counts = block_count[0]
    node_total = node_order.shape[0]
    inverse = (
        jnp.zeros((node_total,), jnp.int32)
        .at[node_order]
        .set(jnp.arange(node_total, dtype=jnp.int32))
    )
    grad_rows_in = out_grad[0]
    full_weight = lax.all_gather(proj_weight, "seq", axis=1, tiled=True)
    upstream = lax.dot_general(
        grad_rows_in, full_weight, (((1,), (1,)), ((), ())), preferred_element_type=jnp.float32
    )
    upstream = upstream.astype(jnp.bfloat16)

    def to_groups(array):
        return array.reshape(nodes_dev, seq_devices, local_heads, head_size)

    query_h = to_groups(queries[0])
    key_h = to_groups(key_vectors[0])
    value_h = to_groups(value_vectors[0])
    upstream_h = to_groups(upstream)
    arrived = (
        lax.all_to_all(query_h, "seq", split_axis=1, concat_axis=0, tiled=True),
        lax.all_to_all(key_h, "seq", split_axis=1, concat_axis=0, tiled=True),
        lax.all_to_all(value_h, "seq", split_axis=1, concat_axis=0, tiled=True),
        lax.all_to_all(upstream_h, "seq", split_axis=1, concat_axis=0, tiled=True),
    )

    def to_cluster(array):
        return jnp.moveaxis(array[:, 0][node_order], 1, 0)

    def single_head(arrays):
        return head_pass(
            arrays[0], arrays[1], arrays[2], arrays[3], col_blocks, block_counts, score_scale
        )

    results = lax.map(single_head, tuple((to_cluster(array) for array in arrived)))
    attn_h, grad_q_h, grad_k_h, grad_v_h = tuple(
        (jnp.moveaxis(array[:, inverse], 0, 1)[:, None] for array in results)
    )
    attn_n, grad_q_n, grad_k_n, grad_v_n = (
        lax.all_to_all(attn_h, "seq", split_axis=0, concat_axis=1, tiled=True),
        lax.all_to_all(grad_q_h, "seq", split_axis=0, concat_axis=1, tiled=True),
        lax.all_to_all(grad_k_h, "seq", split_axis=0, concat_axis=1, tiled=True),
        lax.all_to_all(grad_v_h, "seq", split_axis=0, concat_axis=1, tiled=True),
    )
    attn = attn_n.reshape(nodes_dev, feature_width)
    layer_rows = jnp.dot(attn, full_weight, preferred_element_type=jnp.float32)
    layer_rows = layer_rows.astype(jnp.bfloat16)
    shard_sum = lax.psum_scatter(
        lax.dot_general(
            grad_rows_in, attn, (((0,), (0,)), ((), ())), preferred_element_type=jnp.float32
        ),
        "seq",
        scatter_dimension=0,
        tiled=True,
    )
    shard_sum = lax.psum(shard_sum, "dp")
    weight_shard = shard_sum.T

    def to_rows(array):
        return array.reshape(nodes_dev, feature_width)[None]

    return (layer_rows[None], to_rows(grad_q_n), to_rows(grad_k_n), to_rows(grad_v_n), weight_shard)


def solution(mesh):
    placed = (
        P("dp", "seq", None),
        P("dp", "seq", None),
        P("dp", "seq", None),
        P("dp", "seq", None),
        P(None, "seq"),
        P("dp", None),
        P("dp", None, None),
        P("dp", None),
    )
    return jax.shard_map(
        on_device,
        mesh=mesh,
        in_specs=placed,
        out_specs=(
            P("dp", "seq", None),
            P("dp", "seq", None),
            P("dp", "seq", None),
            P("dp", "seq", None),
            P(None, "seq"),
        ),
        check_vma=False,
    )
```

profile of v0, /device:TPU:1, one launch (start us, length us, event | category | flops | bytes accessed | tf_op | source)
XLA Modules:
  0.0 496.3 jit_solution(6961446493190641195)
XLA Ops:
  9.7 7.6 %all-to-all-start = ((bf16[128,16,1,64]{0,3,2,1:T(8,128)(2,1)}), bf16[128,16,1,64]{0,3,2,1:T(8,128)(2,1)S(1)}, u32[]{:S(2)}, u32[]{:S(2)}) async-start(bf16[128,16,1,64]{0,3,2,1:T(8,128)(2,1)} %bitcast.2), calls=%async_computation | async-start | bytes 524288 | tf_op jit(solution)/shard_map/all_to_all | solution.py:141
  20.9 4.0 all-to-all-done
  24.9 3.5 all-to-all-start.1
  29.1 7.3 %all-to-all-done.1 = bf16[128,16,1,64]{0,3,2,1:T(8,128)(2,1)S(1)} async-done(((bf16[128,16,1,64]{0,3,2,1:T(8,128)(2,1)}), bf16[128,16,1,64]{0,3,2,1:T(8,128)(2,1)S(1)}, u32[]{:S(2)}, u32[]{:S(2)}) %all-to-all-start.1) | async-done | bytes 262176 | tf_op jit(solution)/shard_map/all_to_all | solution.py:142
  36.4 3.5 all-to-all-start.3
  39.9 24.1 %all-gather.2.cloned.1.call-done = bf16[1024,1024]{0,1:T(8,128)(2,1)} async-done(((bf16[1024,64]{0,1:T(8,128)(2,1)}), bf16[1024,1024]{0,1:T(8,128)(2,1)}) %all-gather.2.cloned.1.call-update) | async-done | bytes 2097168 | tf_op jit(solution)/shard_map/all_gather | solution.py:127
  66.9 4.7 all-to-all-start.2
  73.0 8.0 %scatter_custom_fusion = s32[2048]{0:T(1024)S(1)} fusion(s32[2048]{0:T(1024)S(1)} %bitcast.240, s32[2048]{0:T(1024)S(1)} %iota.15, s32[]{:T(128)} %constant.44.clone.1), kind=kCustom, calls=%fused_computation.68 | custom fusion | bytes 8196 | tf_op jit(solution)/shard_map/scatter | solution.py:124
  82.3 8.0 %gather_fusion = bf16[2048,64]{1,0:T(8,128)(2,1)} fusion(bf16[2048,64]{1,0:T(8,128)(2,1)S(1)} %bitcast.208, s32[2048]{0:T(1024)S(1)} %broadcast_clamp_fusion), kind=kCustom, calls=%fused_computation | custom fusion | bytes 532480 | tf_op jit(solution)/shard_map/gather | solution.py:148
  90.3 6.2 %gather_fusion.1 = bf16[2048,64]{1,0:T(8,128)(2,1)S(1)} fusion(bf16[2048,64]{1,0:T(8,128)(2,1)S(1)} %bitcast.209, s32[2048]{0:T(1024)S(1)} %broadcast_clamp_fusion), kind=kCustom, calls=%fused_computation.1 | custom fusion | bytes 532480 | tf_op jit(solution)/shard_map/gather | solution.py:148
  97.9 6.2 %gather_fusion.3 = bf16[2048,64]{1,0:T(8,128)(2,1)S(1)} fusion(bf16[2048,64]{1,0:T(8,128)(2,1)S(1)} %bitcast.211, s32[2048]{0:T(1024)S(1)} %broadcast_clamp_fusion), kind=kCustom, calls=%fused_computation.3 | custom fusion | bytes 532480 | tf_op jit(solution)/shard_map/gather | solution.py:148
  105.5 8.0 %gather_fusion.2 = bf16[2048,64]{1,0:T(8,128)(2,1)} fusion(bf16[2048,64]{1,0:T(8,128)(2,1)S(1)} %bitcast.210, s32[2048]{0:T(1024)S(1)} %broadcast_clamp_fusion), kind=kCustom, calls=%fused_computation.2 | custom fusion | bytes 532480 | tf_op jit(solution)/shard_map/gather | solution.py:148
  113.5 144.4 %while.30 = (s32[]{:T(128)}, f32[32,4096]{1,0:T(8,128)}, f32[32,4096]{1,0:T(8,128)}, bf16[4,8,64,64]{3,2,1,0:T(8,128)(2,1)}, bf16[4,8,64,64]{3,2,1,0:T(8,128)(2,...) while((s32[]{:T(128)}, f32[32,4096]{1,0:T(8,128)}, ...), condition=%wide.region_4.5_spmd.clone, body=%wide.region_0.4_spmd.clone.sunk | while | flops 887306880 | bytes 71800816 | solution.py:89
  118.8 3.3 reshape.301
  129.8 2.7 fusion.96
  132.5 5.0 %reshape.304 = f32[8,16,4096]{2,1,0:T(8,128)} reshape(f32[8,16,64,64]{3,2,1,0:T(8,128)} %fusion.96) | data formatting | bytes 4194304 | tf_op jit(solution)/shard_map/while/body/eval_jaxpr/while/body/eval_jaxpr/reshape | solution.py:80
  140.7 3.5 fusion.94
  144.3 3.6 reshape.303
  154.9 3.3 reshape.301
  165.9 2.7 fusion.96
  168.6 5.0 %reshape.304 = f32[8,16,4096]{2,1,0:T(8,128)} reshape(f32[8,16,64,64]{3,2,1,0:T(8,128)} %fusion.96) | data formatting | bytes 4194304 | tf_op jit(solution)/shard_map/while/body/eval_jaxpr/while/body/eval_jaxpr/reshape | solution.py:80
  173.6 2.5 fusion.97
  176.8 3.5 fusion.94
  180.4 3.6 reshape.303
  191.0 3.3 reshape.301
  202.0 2.7 fusion.96
  204.7 5.0 %reshape.304 = f32[8,16,4096]{2,1,0:T(8,128)} reshape(f32[8,16,64,64]{3,2,1,0:T(8,128)} %fusion.96) | data formatting | bytes 4194304 | tf_op jit(solution)/shard_map/while/body/eval_jaxpr/while/body/eval_jaxpr/reshape | solution.py:80
  209.7 2.5 fusion.97
  212.9 3.5 fusion.94
  216.5 3.6 reshape.303
  227.1 3.3 reshape.301
  238.1 2.6 fusion.96
  240.8 5.0 %reshape.304 = f32[8,16,4096]{2,1,0:T(8,128)} reshape(f32[8,16,64,64]{3,2,1,0:T(8,128)} %fusion.96) | data formatting | bytes 4194304 | tf_op jit(solution)/shard_map/while/body/eval_jaxpr/while/body/eval_jaxpr/reshape | solution.py:80
  245.8 2.5 fusion.97
  249.0 3.5 fusion.94
  252.6 3.6 reshape.303
  257.9 6.7 %gather_fusion.4 = bf16[2048,64]{1,0:T(8,128)(2,1)S(1)} fusion(bf16[2048,64]{1,0:T(8,128)(2,1)} %bitcast.213, s32[2048]{0:T(1024)S(1)} %copy-done.14), kind=kCustom, calls=%fused_computation.4 | custom fusion | bytes 532480 | tf_op jit(solution)/shard_map/gather | solution.py:157
  266.7 14.0 %all_to_all.120 = bf16[16,2,4096]{2,1,0:T(2,128)(2,1)S(1)} all-to-all(bf16[16,2,4096]{2,1,0:T(2,128)(2,1)S(1)} %reshape.289), channel_id=1, replica_groups=mesh['dp'=16,'seq'=16] {'seq'}, dimensions={0} | all-to-all | bytes 524288 | tf_op jit(solution)/shard_map/all_to_all | solution.py:160
  282.7 2.7 convolution_bitcast_fusion.4
  285.4 5.4 %copy.118 = f32[1024,1024]{1,0:T(8,128)} copy(f32[1024,1024]{0,1:T(8,128)} %convolution_bitcast_fusion.4) | data formatting | bytes 8388608
  292.4 6.2 %gather_fusion.6 = bf16[2048,64]{1,0:T(8,128)(2,1)S(1)} fusion(bf16[2048,64]{1,0:T(8,128)(2,1)S(1)} %reshape.216, s32[2048]{0:T(1024)S(1)} %copy-done.14), kind=kCustom, calls=%fused_computation.6 | custom fusion | bytes 532480 | tf_op jit(solution)/shard_map/gather | solution.py:157
  300.8 3.5 all-to-all-start.6
  305.0 6.2 %gather_fusion.7 = bf16[2048,64]{1,0:T(8,128)(2,1)S(1)} fusion(bf16[2048,64]{1,0:T(8,128)(2,1)S(1)} %reshape.226, s32[2048]{0:T(1024)S(1)} %copy-done.14), kind=kCustom, calls=%fused_computation.7 | custom fusion | bytes 532480 | tf_op jit(solution)/shard_map/gather | solution.py:157
  313.4 6.6 %all-to-all-start.7 = ((bf16[16,2,4096]{2,1,0:T(2,128)(2,1)}), bf16[16,2,4096]{2,1,0:T(2,128)(2,1)S(1)}, u32[]{:S(2)}, u32[]{:S(2)}) async-start(bf16[16,2,4096]{2,1,0:T(2,128)(2,1)} %reshape.295), calls=%async_computation.7 | async-start | bytes 524288 | tf_op jit(solution)/shard_map/all_to_all | solution.py:163
  320.0 6.2 %gather_fusion.5 = bf16[2048,64]{1,0:T(8,128)(2,1)S(1)} fusion(bf16[2048,64]{1,0:T(8,128)(2,1)S(1)} %bitcast.212, s32[2048]{0:T(1024)S(1)} %copy-done.14), kind=kCustom, calls=%fused_computation.5 | custom fusion | bytes 532480 | tf_op jit(solution)/shard_map/gather | solution.py:157
  328.4 6.7 %all-to-all-start.5 = ((bf16[16,2,4096]{2,1,0:T(2,128)(2,1)}), bf16[16,2,4096]{2,1,0:T(2,128)(2,1)}, u32[]{:S(2)}, u32[]{:S(2)}) async-start(bf16[16,2,4096]{2,1,0:T(2,128)(2,1)} %reshape.291), calls=%async_computation.5 | async-start | bytes 524288 | tf_op jit(solution)/shard_map/all_to_all | solution.py:161
  348.9 25.9 %reduce-scatter.4.cloned.1.call-done = f32[64,1024]{1,0:T(8,128)} async-done(((f32[1024,1024]{1,0:T(8,128)}), f32[64,1024]{1,0:T(8,128)}) %reduce-scatter.4.cloned.1.call-update) | async-done | bytes 262160
  379.2 108.7 %all-reduce.2.cloned.1.call-done = f32[1024,64]{1,0:T(8,128)} async-done(((f32[1024,64]{1,0:T(8,128)}), f32[1024,64]{1,0:T(8,128)}) %all-reduce.2.cloned.1.call-update) | async-done | bytes 262160 | tf_op jit(solution)/shard_map/psum | solution.py:176
  (204 shorter events, 112.3 us)
Async XLA Ops:
  7.2 56.9 %copy-start = (bf16[1,128,1024]{2,1,0:T(8,128)(2,1)S(1)}, bf16[1,128,1024]{2,1,0:T(8,128)(2,1)}, u32[]{:S(2)}) copy-start(bf16[1,128,1024]{2,1,0:T(8,128)(2,1)} %param.13) | copy-start | bytes 786436
  7.2 65.0 %copy-start.16 = (s32[1,32]{1,0:T(1,128)S(1)}, s32[1,32]{1,0:T(1,128)}, u32[]{:S(2)}) copy-start(s32[1,32]{1,0:T(1,128)} %param.17) | copy-start | bytes 388
  7.2 73.8 %copy-start.15 = (s32[1,32,16]{1,2,0:T(8,128)S(1)}, s32[1,32,16]{1,2,0:T(8,128)}, u32[]{:S(2)}) copy-start(s32[1,32,16]{1,2,0:T(8,128)} %param.16) | copy-start | bytes 6148
  7.2 56.8 %all-gather.2.cloned.1.call-start = ((), (), s32[]{:S(2)}) async-start(), calls=%async_computation.9 | async-start | bytes 2228224 | tf_op jit(solution)/shard_map/all_gather | solution.py:127
  9.7 15.1 %all-to-all-start = ((bf16[128,16,1,64]{0,3,2,1:T(8,128)(2,1)}), bf16[128,16,1,64]{0,3,2,1:T(8,128)(2,1)S(1)}, u32[]{:S(2)}, u32[]{:S(2)}) async-start(bf16[128,16,1,64]{0,3,2,1:T(8,128)(2,1)} %bitcast.2), calls=%async_computation | async-start | bytes 524288 | tf_op jit(solution)/shard_map/all_to_all | solution.py:141
  24.9 11.5 %all-to-all-start.1 = ((bf16[128,16,1,64]{0,3,2,1:T(8,128)(2,1)}), bf16[128,16,1,64]{0,3,2,1:T(8,128)(2,1)S(1)}, u32[]{:S(2)}, u32[]{:S(2)}) async-start(bf16[128,16,1,64]{0,3,2,1:T(8,128)(2,1)} %bitcast.10), calls=%async_computation.1 | async-start | bytes 524288 | tf_op jit(solution)/shard_map/all_to_all | solution.py:142
  36.4 30.5 %all-to-all-start.3 = ((bf16[128,16,1,64]{0,3,2,1:T(8,128)(2,1)}), bf16[128,16,1,64]{0,3,2,1:T(8,128)(2,1)S(1)}, u32[]{:S(2)}, u32[]{:S(2)}) async-start(bf16[128,16,1,64]{0,3,2,1:T(8,128)(2,1)} %bitcast.22), calls=%async_computation.3 | async-start | bytes 524288 | tf_op jit(solution)/shard_map/all_to_all | solution.py:143
  66.9 38.3 %all-to-all-start.2 = ((bf16[128,16,1,64]{0,3,2,1:T(8,128)(2,1)}), bf16[128,16,1,64]{0,3,2,1:T(8,128)(2,1)S(1)}, u32[]{:S(2)}, u32[]{:S(2)}) async-start(bf16[128,16,1,64]{0,3,2,1:T(8,128)(2,1)} %bitcast.16), calls=%async_computation.2 | async-start | bytes 524288 | tf_op jit(solution)/shard_map/all_to_all | solution.py:144
  71.6 303.1 %reduce-scatter.4.cloned.1.call-start = ((), (), s32[]{:S(2)}) async-start(), calls=%async_computation.11 | async-start | bytes 4456448
  113.5 144.4 %copy-start.14 = (s32[2048]{0:T(1024)S(1)}, s32[2048]{0:T(1024)}, u32[]{:S(2)}) copy-start(s32[2048]{0:T(1024)} %fusion.40) | copy-start | bytes 24580
  122.1 2.9 copy-start.3
  122.1 2.9 copy-start.13
  128.3 1.5 copy-start.1
  132.5 5.0 %copy-start.5 = (f32[32,4096]{1,0:T(8,128)S(1)}, f32[32,4096]{1,0:T(8,128)}, u32[]{:S(2)}) copy-start(f32[32,4096]{1,0:T(8,128)} %get-tuple-element.281) | copy-start | bytes 1572868 | tf_op jit(solution)/shard_map/while/body/eval_jaxpr/while
  132.5 8.2 %copy-start.2 = (bf16[8,64,16,64]{1,3,2,0:T(8,128)(2,1)S(1)}, bf16[8,64,16,64]{1,3,2,0:T(8,128)(2,1)}, u32[]{:S(2)}) copy-start(bf16[8,64,16,64]{1,3,2,0:T(8,128)(2,1)} %copy-done.1) | copy-start | bytes 3145732 | tf_op jit(solution)/shard_map/while/body/eval_jaxpr/while
  140.0 7.9 %copy-start.6 = (f32[32,4096]{1,0:T(8,128)}, f32[32,4096]{1,0:T(8,128)S(1)}, u32[]{:S(2)}) copy-start(f32[32,4096]{1,0:T(8,128)S(1)} %fusion.97) | copy-start | bytes 1572868 | tf_op jit(solution)/shard_map/while/body/eval_jaxpr/while
  144.2 3.6 copy-start.8
  148.8 0.8 copy-start.9
  158.2 2.9 copy-start.3
  158.2 2.9 copy-start.13
  164.4 1.5 copy-start.1
  168.6 5.0 %copy-start.5 = (f32[32,4096]{1,0:T(8,128)S(1)}, f32[32,4096]{1,0:T(8,128)}, u32[]{:S(2)}) copy-start(f32[32,4096]{1,0:T(8,128)} %get-tuple-element.281) | copy-start | bytes 1572868 | tf_op jit(solution)/shard_map/while/body/eval_jaxpr/while
  168.6 8.2 %copy-start.2 = (bf16[8,64,16,64]{1,3,2,0:T(8,128)(2,1)S(1)}, bf16[8,64,16,64]{1,3,2,0:T(8,128)(2,1)}, u32[]{:S(2)}) copy-start(bf16[8,64,16,64]{1,3,2,0:T(8,128)(2,1)} %copy-done.1) | copy-start | bytes 3145732 | tf_op jit(solution)/shard_map/while/body/eval_jaxpr/while
  176.1 7.9 %copy-start.6 = (f32[32,4096]{1,0:T(8,128)}, f32[32,4096]{1,0:T(8,128)S(1)}, u32[]{:S(2)}) copy-start(f32[32,4096]{1,0:T(8,128)S(1)} %fusion.97) | copy-start | bytes 1572868 | tf_op jit(solution)/shard_map/while/body/eval_jaxpr/while
  180.4 3.6 copy-start.8
  184.9 0.8 copy-start.9
  194.3 2.9 copy-start.3
  194.3 2.9 copy-start.13
  200.6 1.5 copy-start.1
  204.7 5.0 %copy-start.5 = (f32[32,4096]{1,0:T(8,128)S(1)}, f32[32,4096]{1,0:T(8,128)}, u32[]{:S(2)}) copy-start(f32[32,4096]{1,0:T(8,128)} %get-tuple-element.281) | copy-start | bytes 1572868 | tf_op jit(solution)/shard_map/while/body/eval_jaxpr/while
  204.7 8.2 %copy-start.2 = (bf16[8,64,16,64]{1,3,2,0:T(8,128)(2,1)S(1)}, bf16[8,64,16,64]{1,3,2,0:T(8,128)(2,1)}, u32[]{:S(2)}) copy-start(bf16[8,64,16,64]{1,3,2,0:T(8,128)(2,1)} %copy-done.1) | copy-start | bytes 3145732 | tf_op jit(solution)/shard_map/while/body/eval_jaxpr/while
  212.2 7.9 %copy-start.6 = (f32[32,4096]{1,0:T(8,128)}, f32[32,4096]{1,0:T(8,128)S(1)}, u32[]{:S(2)}) copy-start(f32[32,4096]{1,0:T(8,128)S(1)} %fusion.97) | copy-start | bytes 1572868 | tf_op jit(solution)/shard_map/while/body/eval_jaxpr/while
  216.5 3.6 copy-start.8
  230.4 2.9 copy-start.3
  230.4 2.9 copy-start.13
  236.7 1.5 copy-start.1
  240.8 5.0 %copy-start.5 = (f32[32,4096]{1,0:T(8,128)S(1)}, f32[32,4096]{1,0:T(8,128)}, u32[]{:S(2)}) copy-start(f32[32,4096]{1,0:T(8,128)} %get-tuple-element.281) | copy-start | bytes 1572868 | tf_op jit(solution)/shard_map/while/body/eval_jaxpr/while
  240.8 8.2 %copy-start.2 = (bf16[8,64,16,64]{1,3,2,0:T(8,128)(2,1)S(1)}, bf16[8,64,16,64]{1,3,2,0:T(8,128)(2,1)}, u32[]{:S(2)}) copy-start(bf16[8,64,16,64]{1,3,2,0:T(8,128)(2,1)} %copy-done.1) | copy-start | bytes 3145732 | tf_op jit(solution)/shard_map/while/body/eval_jaxpr/while
  248.3 7.8 %copy-start.6 = (f32[32,4096]{1,0:T(8,128)}, f32[32,4096]{1,0:T(8,128)S(1)}, u32[]{:S(2)}) copy-start(f32[32,4096]{1,0:T(8,128)S(1)} %fusion.97) | copy-start | bytes 1572868 | tf_op jit(solution)/shard_map/while/body/eval_jaxpr/while
  252.6 3.6 copy-start.8
  290.8 1.0 copy-start.10
  291.8 12.5 %copy-start.7 = (f32[32,4096]{1,0:T(8,128)S(1)}, f32[32,4096]{1,0:T(8,128)}, u32[]{:S(2)}) copy-start(f32[32,4096]{1,0:T(8,128)} %get-tuple-element.106) | copy-start | bytes 1572868
  300.8 12.6 %all-to-all-start.6 = ((bf16[16,2,4096]{2,1,0:T(2,128)(2,1)}), bf16[16,2,4096]{2,1,0:T(2,128)(2,1)S(1)}, u32[]{:S(2)}, u32[]{:S(2)}) async-start(bf16[16,2,4096]{2,1,0:T(2,128)(2,1)} %reshape.293), calls=%async_computation.6 | async-start | bytes 524288 | tf_op jit(solution)/shard_map/all_to_all | solution.py:162
  304.4 15.6 %copy-start.4 = (bf16[4,8,64,64]{3,2,1,0:T(8,128)(2,1)S(1)}, bf16[4,8,64,64]{3,2,1,0:T(8,128)(2,1)}, u32[]{:S(2)}) copy-start(bf16[4,8,64,64]{3,2,1,0:T(8,128)(2,1)} %get-tuple-element.104) | copy-start | bytes 786436
  313.4 15.0 %all-to-all-start.7 = ((bf16[16,2,4096]{2,1,0:T(2,128)(2,1)}), bf16[16,2,4096]{2,1,0:T(2,128)(2,1)S(1)}, u32[]{:S(2)}, u32[]{:S(2)}) async-start(bf16[16,2,4096]{2,1,0:T(2,128)(2,1)} %reshape.295), calls=%async_computation.7 | async-start | bytes 524288 | tf_op jit(solution)/shard_map/all_to_all | solution.py:163
  328.4 14.7 %all-to-all-start.5 = ((bf16[16,2,4096]{2,1,0:T(2,128)(2,1)}), bf16[16,2,4096]{2,1,0:T(2,128)(2,1)}, u32[]{:S(2)}, u32[]{:S(2)}) async-start(bf16[16,2,4096]{2,1,0:T(2,128)(2,1)} %reshape.291), calls=%async_computation.5 | async-start | bytes 524288 | tf_op jit(solution)/shard_map/all_to_all | solution.py:161
  335.1 152.7 %all-reduce.2.cloned.1.call-start = ((), (), s32[]{:S(2)}) async-start(), calls=%async_computation.10 | async-start | bytes 1048576 | tf_op jit(solution)/shard_map/psum | solution.py:176
  338.0 38.7 %copy-start.11 = (bf16[1024,1024]{0,1:T(8,128)(2,1)S(1)}, bf16[1024,1024]{0,1:T(8,128)(2,1)}, u32[]{:S(2)}) copy-start(bf16[1024,1024]{0,1:T(8,128)(2,1)} %all-gather.2.cloned.1.call-done) | copy-start | bytes 6291460
  (3 other events, 2.3 us)
Sparse Core Ops, SparseCore 0:
  10.5 53.5 all-gather.1
  290.9 83.7 reduce-scatter.3
  377.1 110.6 all-reduce.1
where the time goes:
time: 498 us; the launch traced here: 496 us
  waiting for transfers between devices  172 us (35%)
  local copies, waits for them, and re-layouts  164 us (33%)
  matrix products  83.7 us (17%)
  starting transfers between devices  36.3 us (7%)
  between operations  14.2 us (3%)
  blocking collectives  14 us (3%)
  other arithmetic  11.2 us (2%)
    psum x1, waiting for transfers between devices, on_device(): shard_sum = lax.psum(shard_sum, 'dp')  109 us
    unnamed x41, local copies, waits for them, and re-layouts  29.3 us
    gather x4, local copies, waits for them, and re-layouts, to_cluster(): return jnp.moveaxis(array[:, 0][node_order], 1, 0)  28.3 us
    unnamed x4, waiting for transfers between devices  26.6 us
    gather x4, local copies, waits for them, and re-layouts, on_device(): array[:, inverse]  25.3 us
    all_gather x1, waiting for transfers between devices, on_device(): full_weight = lax.all_gather(proj_weight, 'seq', axis=1, tiled=True)  24.1 us
    reshape x4, local copies, waits for them, and re-layouts, group_step(): value_terms.reshape(row_blocks, list_len, tile_width)  19.9 us
    reshape x4, local copies, waits for them, and re-layouts, group_step(): key_terms.reshape(row_blocks, list_len, tile_width)  14.3 us
  transfers between devices with their start and end apart: 10, of which 6 were waited for; matrix products, arithmetic and copies ran while one was open for 17% of the time, Pallas kernels for 0%

commit v1 on v0

v1 whole, which is shorter than its diff:
```python
import functools
import jax
import jax.numpy as jnp
from jax import lax
from jax.experimental import pallas as pl
from jax.experimental.pallas import tpu as pltpu
from jax.sharding import PartitionSpec as P

BLK = 64
F32 = jnp.float32
BF16 = jnp.bfloat16


def attention_kernel(
    cols_ref, count_ref, qb_in, kv_in, order_ref, oq_out, dkv_out,
    qb_ref, kv_ref, kvt_ref, score_ref, gsm_ref, acc_ref, oq_ref,
):
    nodes = qb_in.shape[0]
    nblk = nodes // BLK
    listed = cols_ref.shape[1]
    pairs = nblk // 2
    chunks = listed // 4
    order_col = jnp.transpose(
        jnp.concatenate(
            [order_ref[...].astype(F32),
             jnp.zeros((128 - order_ref.shape[0], 128), F32)], axis=0)
    ).astype(jnp.int32)
    lane_node = lax.broadcasted_iota(jnp.int32, (128, nodes), 1)
    low = lax.broadcasted_iota(jnp.int32, (128, 128), 1) < BLK
    zero = jnp.zeros((128, 128), BF16)
    rows = jnp.concatenate([qb_in[...], kv_in[...]], axis=1)
    for i in range(nodes // 128):
        pick = (lane_node == order_col[:, i:i + 1]).astype(F32).astype(BF16)
        moved = jnp.dot(pick, rows, preferred_element_type=F32)
        qb = moved[:, :128]
        qb_ref[i * 128:(i + 1) * 128, :] = jnp.where(low, qb * 0.125, qb).astype(BF16)
        kv = moved[:, 128:].astype(BF16)
        kv_ref[2 * i] = kv[:BLK]
        kv_ref[2 * i + 1] = kv[BLK:]
        kvt = jnp.transpose(moved[:, 128:])
        swap = pltpu.roll(kvt, BLK, 1)
        kvt = kvt.astype(BF16)
        swap = swap.astype(BF16)
        kvt_ref[0, 2 * i] = jnp.where(low, kvt, zero)
        kvt_ref[1, 2 * i] = jnp.where(low, zero, swap)
        kvt_ref[0, 2 * i + 1] = jnp.where(low, swap, zero)
        kvt_ref[1, 2 * i + 1] = jnp.where(low, zero, kvt)
    acc_ref[...] = jnp.zeros_like(acc_ref)

    lane = lax.broadcasted_iota(jnp.int32, (1, 128), 1)
    low64 = lax.broadcasted_iota(jnp.int32, (BLK, 128), 1) < BLK
    zero64 = jnp.zeros((BLK, 128), BF16)

    def pair_step(i, carry):
        first = 2 * i
        second = first + 1
        qb1 = qb_ref[pl.ds(pl.multiple_of(i * 128, 128), BLK), :]
        qb2 = qb_ref[pl.ds(pl.multiple_of(i * 128 + BLK, BLK), BLK), :]
        weights = jnp.concatenate(
            [
                jnp.concatenate([jnp.where(low64, qb1, zero64), zero64], axis=1),
                jnp.concatenate([zero64, jnp.where(low64, qb2, zero64)], axis=1),
                jnp.concatenate([jnp.where(low64, zero64, qb1), zero64], axis=1),
                jnp.concatenate([zero64, jnp.where(low64, zero64, qb2)], axis=1),
            ],
            axis=0,
        )
        live = jnp.where(lane < BLK, count_ref[first], count_ref[second])
        peak = jnp.full((8, 128), -jnp.inf, F32)
        for c in range(chunks):
            lhs = jnp.concatenate(
                [
                    jnp.concatenate(
                        [kv_ref[cols_ref[first, m]], kv_ref[cols_ref[second, m]]], axis=1)
                    for m in range(4 * c, 4 * c + 4)
                ],
                axis=0,
            )
            both = lax.dot_general(
                lhs, weights, (((1,), (1,)), ((), ())), preferred_element_type=F32)
            for k in range(4):
                m = 4 * c + k
                part = jnp.where(m < live, both[k * BLK:(k + 1) * BLK, :128], -jnp.inf)
                score_ref[m * BLK:(m + 1) * BLK, :] = part
                peak = jnp.maximum(peak, jnp.max(part.reshape(8, 8, 128), axis=0))
            gsm_ref[c * 256:(c + 1) * 256, :] = both[:, 128:]
        peak = jnp.max(peak, axis=0, keepdims=True)
        total = jnp.zeros((8, 128), F32)
        delta = jnp.zeros((8, 128), F32)
        for c in range(chunks):
            rows = slice(c * 256, (c + 1) * 256)
            terms = jnp.exp(score_ref[rows, :] - peak)
            score_ref[rows, :] = terms
            total = total + jnp.sum(terms.reshape(32, 8, 128), axis=0)
            delta = delta + jnp.sum((terms * gsm_ref[rows, :]).reshape(32, 8, 128), axis=0)
        inv = 1.0 / jnp.sum(total, axis=0, keepdims=True)
        delta = jnp.sum(delta, axis=0, keepdims=True) * inv
        back = jnp.zeros((256, 256), F32)
        swapped = jnp.concatenate([weights[128:], weights[:128]], axis=0)
        for c in range(chunks):
            rows = slice(c * 256, (c + 1) * 256)
            soft = score_ref[rows, :] * inv
            grad = soft * (gsm_ref[rows, :] - delta)
            both = jnp.concatenate([soft.astype(BF16), grad.astype(BF16)], axis=1)
            key_terms = jnp.dot(both, swapped, preferred_element_type=F32)
            for k in range(4):
                m = 4 * c + k
                acc_ref[cols_ref[first, m]] += key_terms[k * BLK:(k + 1) * BLK, :128]
                acc_ref[cols_ref[second, m]] += key_terms[k * BLK:(k + 1) * BLK, 128:]
            sides = []
            for row in (first, second):
                sides.append(jnp.concatenate(
                    [
                        kvt_ref[0, cols_ref[row, m]] + kvt_ref[1, cols_ref[row, m + 1]]
                        for m in range(4 * c, 4 * c + 4, 2)
                    ],
                    axis=1,
                ))
            back = back + jnp.dot(
                jnp.concatenate(sides, axis=0), both, preferred_element_type=F32)
        outputs = jnp.where(low64, back[BLK:128, :128], back[128 + BLK:, :128])
        grad_q = jnp.where(low64, back[:BLK, 128:], back[128:128 + BLK, 128:]) * 0.125
        here = pl.ds(pl.multiple_of(i * 128, 128), 128)
        oq_ref[:BLK, here] = outputs.astype(BF16)
        oq_ref[BLK:, here] = grad_q.astype(BF16)
        return carry

    lax.fori_loop(0, pairs, pair_step, 0)

    order_row = jnp.concatenate([order_ref[i:i + 1, :] for i in range(nodes // 128)], axis=1)
    grad_kv = acc_ref[...].reshape(nodes, 128).astype(BF16)
    for j in range(nodes // 128):
        row_node = lax.broadcasted_iota(jnp.int32, (128, nodes), 0) + j * 128
        pick = (row_node == order_row).astype(F32).astype(BF16)
        oq_out[j] = lax.dot_general(
            pick, oq_ref[...], (((1,), (1,)), ((), ())), preferred_element_type=F32).astype(BF16)
        dkv_out[j] = jnp.dot(pick, grad_kv, preferred_element_type=F32).astype(BF16)


def attention(qb, kv, order, cols, count):
    nodes = qb.shape[0]
    nblk, listed = cols.shape
    smem = pl.BlockSpec(memory_space=pltpu.SMEM)
    vmem = pl.BlockSpec(memory_space=pltpu.VMEM)
    return pl.pallas_call(
        attention_kernel,
        out_shape=(jax.ShapeDtypeStruct((nodes // 128, 128, 128), BF16),) * 2,
        in_specs=[smem, smem, vmem, vmem, vmem],
        out_specs=(vmem, vmem),
        scratch_shapes=[
            pltpu.VMEM((nodes, 128), BF16),
            pltpu.VMEM((nblk, BLK, 128), BF16),
            pltpu.VMEM((2, nblk, 128, 128), BF16),
            pltpu.VMEM((listed * BLK, 128), F32),
            pltpu.VMEM((listed * BLK, 128), F32),
            pltpu.VMEM((nblk, BLK, 128), F32),
            pltpu.VMEM((128, nodes), BF16),
        ],
        compiler_params=pltpu.CompilerParams(vmem_limit_bytes=48 * 1024 * 1024),
        name="head_attention",
    )(cols, count, qb, kv, order.reshape(nodes // 128, 128))

MESH = pl.DeviceIdType.MESH
SIDE = 4


def greet(devices):
    barrier = pltpu.get_barrier_semaphore()
    for device in devices:
        pl.semaphore_signal(barrier, inc=1, device_id=device, device_id_type=MESH)
    pl.semaphore_wait(barrier, len(devices))


def push(src, dst, send_sem, recv_sem, device):
    copy = pltpu.make_async_remote_copy(
        src_ref=src, dst_ref=dst, send_sem=send_sem, recv_sem=recv_sem,
        device_id=device, device_id_type=MESH)
    copy.start()
    return copy


def beside(a, b):
    return jnp.concatenate([a, b], axis=1)


def inward_kernel(
    q_ref, k_ref, v_ref, g_ref, w_ref, qb_ref, kv_ref, wt_ref,
    up_ref, qb_out, kv_out,
    w1_send, w1_recv, w2_send, w2_recv, core_send, core_recv,
    kv_send, kv_recv, qb_send, qb_recv,
):
    dp, me = lax.axis_index("dp"), lax.axis_index("seq")
    seq = kv_ref.shape[0]
    y, x = me // SIDE, me % SIDE
    core = dp % 2
    mate = (dp + 1 - 2 * core, me)
    peers = [lax.rem(me + i, seq) for i in range(1, seq)]
    xs = [(y, lax.rem(x + i, SIDE)) for i in range(1, SIDE)]
    ys = [(lax.rem(y + i, SIDE), x) for i in range(1, SIDE)]
    x_peers = [(dp, y * SIDE + at) for _, at in xs]
    y_peers = [(dp, at * SIDE + x) for at, _ in ys]
    greet([(dp, p) for p in peers] + [mate])

    share = w_ref.shape[1]
    rows = share // 4
    eye = (lax.broadcasted_iota(jnp.int32, (share, share), 0)
           == lax.broadcasted_iota(jnp.int32, (share, share), 1)).astype(jnp.float32)
    wt_ref[y, x] = lax.dot_general(
        eye.astype(jnp.bfloat16), w_ref[...], (((1,), (1,)), ((), ())),
        preferred_element_type=jnp.float32).astype(jnp.bfloat16)
    start_a = pl.multiple_of(core * 2 * rows, 2 * rows)
    half_a = pl.ds(start_a, rows)
    half_b = pl.ds(pl.multiple_of(start_a + rows, rows), rows)
    first = []
    for i in range(SIDE - 1):
        for n, (part, targets) in enumerate(((half_a, x_peers), (half_b, y_peers))):
            piece = wt_ref.at[y, x, part]
            first.append(push(piece, piece, w1_send.at[n, i], w1_recv.at[n, i], targets[i]))

    width = 64
    for j in range(seq // 2):
        lanes = slice(2 * width * j, 2 * width * (j + 1))
        k, v = k_ref[:, lanes], v_ref[:, lanes]
        kv_out[2 * j] = beside(k[:, :width], v[:, :width])
        kv_out[2 * j + 1] = beside(k[:, width:], v[:, width:])
    kv_ref[me] = kv_out[me]
    kv_copies = [
        push(kv_out.at[p], kv_ref.at[me], kv_send.at[i], kv_recv.at[i], (dp, p))
        for i, p in enumerate(peers)]

    second, across = [], []
    for copy in first:
        copy.wait_recv()
    for i in range(SIDE - 1):
        for n, (part, sources) in enumerate(((half_a, xs), (half_b, ys))):
            piece = wt_ref.at[sources[i][0], sources[i][1], part]
            across.append(push(piece, piece, core_send.at[n, i], core_recv.at[n, i], mate))
    for i in range(SIDE - 1):
        piece = wt_ref.at[y, :, half_a]
        second.append(push(piece, piece, w2_send.at[0, i], w2_recv.at[0, i], y_peers[i]))
        piece = wt_ref.at[:, x, half_b]
        second.append(push(piece, piece, w2_send.at[1, i], w2_recv.at[1, i], x_peers[i]))
    for i in range(SIDE - 1):
        back = SIDE - 1 - i
        second[2 * i].wait_recv()
        piece = wt_ref.at[lax.rem(y + back, SIDE), :, half_a]
        across.append(push(piece, piece, core_send.at[2, i], core_recv.at[2, i], mate))
        second[2 * i + 1].wait_recv()
        piece = wt_ref.at[:, lax.rem(x + back, SIDE), half_b]
        across.append(push(piece, piece, core_send.at[3, i], core_recv.at[3, i], mate))
    for copy in across:
        copy.wait_recv()

    up_ref[...] = jnp.dot(
        g_ref[...], wt_ref[...].reshape(seq * share, wt_ref.shape[3]),
        preferred_element_type=jnp.float32).astype(jnp.bfloat16)
    for j in range(seq // 2):
        lanes = slice(2 * width * j, 2 * width * (j + 1))
        q, b = q_ref[:, lanes], up_ref[:, lanes]
        qb_out[2 * j] = beside(q[:, :width], b[:, :width])
        qb_out[2 * j + 1] = beside(q[:, width:], b[:, width:])
    qb_ref[me] = qb_out[me]
    qb_copies = [
        push(qb_out.at[p], qb_ref.at[me], qb_send.at[i], qb_recv.at[i], (dp, p))
        for i, p in enumerate(peers)]
    for copy in kv_copies + qb_copies:
        copy.wait_recv()
    for copy in first + second + across + kv_copies + qb_copies:
        copy.wait_send()


def inward(queries, keys, values, grads, weight, seq):
    nodes, depth = queries.shape
    share = weight.shape[1]
    vmem = pl.BlockSpec(memory_space=pltpu.VMEM)
    dma = pltpu.SemaphoreType.DMA
    bf16 = jnp.bfloat16
    side = SIDE - 1
    return pl.pallas_call(
        inward_kernel,
        out_shape=(
            jax.ShapeDtypeStruct((seq, nodes, 128), bf16),
            jax.ShapeDtypeStruct((seq, nodes, 128), bf16),
            jax.ShapeDtypeStruct((SIDE, SIDE, share, depth), bf16),
        ),
        in_specs=[vmem] * 5,
        out_specs=(vmem,) * 3,
        scratch_shapes=[
            pltpu.VMEM((nodes, depth), bf16),
            pltpu.VMEM((seq, nodes, 128), bf16),
            pltpu.VMEM((seq, nodes, 128), bf16),
            dma((2, side)), dma((2, side)), dma((2, side)), dma((2, side)),
            dma((4, side)), dma((4, side)),
            dma((seq - 1,)), dma((seq - 1,)), dma((seq - 1,)), dma((seq - 1,)),
        ],
        compiler_params=pltpu.CompilerParams(
            collective_id=0, has_side_effects=True, vmem_limit_bytes=48 * 1024 * 1024),
        name="inward",
    )(queries, keys, values, grads, weight)


def outward_kernel(
    oq_ref, kv_ref, g_ref, wt_ref,
    layer_ref, dq_ref, dk_ref, dv_ref, wg_ref,
    oq_in, kv_in, attn_ref, part_ref, mate_out, mate_in,
    sum_ref, half_ref, line_in, cross_out, cross_in, z_out, z_in, all_in,
    oq_send, oq_recv, kv_send, kv_recv, mate_send, mate_recv,
    line_send, line_recv, cross_send, cross_recv, z_send, z_recv, all_send, all_recv,
):
    dp, me = lax.axis_index("dp"), lax.axis_index("seq")
    seq = oq_ref.shape[0]
    dps = all_in.shape[0]
    nz = dps // 2
    f32, bf16 = jnp.float32, jnp.bfloat16
    y, x = me // SIDE, me % SIDE
    core, z = dp % 2, dp // 2
    mate = (dp + 1 - 2 * core, me)
    peers = [lax.rem(me + i, seq) for i in range(1, seq)]
    dp_peers = [lax.rem(dp + i, dps) for i in range(1, dps)]
    z_peers = [lax.rem(z + i, nz) for i in range(1, nz)]
    xs = [lax.rem(x + i, SIDE) for i in range(1, SIDE)]
    ys = [lax.rem(y + i, SIDE) for i in range(1, SIDE)]
    greet([(dp, p) for p in peers] + [(p, me) for p in dp_peers])

    oq_in[me] = oq_ref[me]
    oq_copies = [
        push(oq_ref.at[p], oq_in.at[me], oq_send.at[i], oq_recv.at[i], (dp, p))
        for i, p in enumerate(peers)]
    kv_in[me] = kv_ref[me]
    kv_copies = [
        push(kv_ref.at[p], kv_in.at[me], kv_send.at[i], kv_recv.at[i], (dp, p))
        for i, p in enumerate(peers)]

    width = 64
    for copy in oq_copies:
        copy.wait_recv()
    for j in range(seq // 2):
        lanes = slice(2 * width * j, 2 * width * (j + 1))
        a, b = oq_in[2 * j], oq_in[2 * j + 1]
        attn_ref[:, lanes] = beside(a[:, :width], b[:, :width])
        dq_ref[:, lanes] = beside(a[:, width:], b[:, width:])

    depth = attn_ref.shape[1]
    share = depth // seq
    keep = pl.ds(pl.multiple_of(core * (share // 2), share // 2), share // 2)
    give = pl.ds(pl.multiple_of((1 - core) * (share // 2), share // 2), share // 2)
    mate_copies = []
    for c in range(SIDE):
        part_ref[c] = lax.dot_general(
            g_ref[:, c * SIDE * share:(c + 1) * SIDE * share], attn_ref[...],
            (((0,), (0,)), ((), ())), preferred_element_type=f32).reshape(SIDE, share, depth)
        mate_out[c] = part_ref[c, :, give, :].astype(bf16)
        mate_copies.append(push(
            mate_out.at[c], mate_in.at[c], mate_send.at[c], mate_recv.at[c], mate))
    layer_ref[...] = lax.dot_general(
        attn_ref[...], wt_ref[...].reshape(depth, depth), (((1,), (1,)), ((), ())),
        preferred_element_type=f32).astype(bf16)
    for c in range(SIDE):
        mate_copies[c].wait_recv()
        total = part_ref[c, :, keep, :] + mate_in[c].astype(f32)
        sum_ref[c] = total
        half_ref[c] = total.astype(bf16)
    rows = share // 4
    line = []
    for i in range(SIDE - 1):
        line.append(push(
            half_ref.at[:, xs[i], :rows], line_in.at[0, i],
            line_send.at[0, i], line_recv.at[0, i], (dp, y * SIDE + xs[i])))
        line.append(push(
            half_ref.at[ys[i], :, rows:], line_in.at[1, i],
            line_send.at[1, i], line_recv.at[1, i], (dp, ys[i] * SIDE + x)))
    for copy in line:
        copy.wait_recv()
    sum_a = sum_ref[:, pl.ds(x, 1), :rows, :].reshape(SIDE, rows, depth)
    sum_b = sum_ref[pl.ds(y, 1), :, rows:, :].reshape(SIDE, rows, depth)
    for i in range(SIDE - 1):
        sum_a += line_in[0, i].astype(f32)
        sum_b += line_in[1, i].astype(f32)
    cross_out[0] = sum_a.astype(bf16)
    cross_out[1] = sum_b.astype(bf16)
    cross = []
    for i in range(SIDE - 1):
        cross.append(push(
            cross_out.at[0, ys[i]], cross_in.at[0, i],
            cross_send.at[0, i], cross_recv.at[0, i], (dp, ys[i] * SIDE + x)))
        cross.append(push(
            cross_out.at[1, xs[i]], cross_in.at[1, i],
            cross_send.at[1, i], cross_recv.at[1, i], (dp, y * SIDE + xs[i])))
    for copy in cross:
        copy.wait_recv()
    shard_a = cross_out[0, y].astype(f32)
    shard_b = cross_out[1, x].astype(f32)
    for i in range(SIDE - 1):
        shard_a += cross_in[0, i].astype(f32)
        shard_b += cross_in[1, i].astype(f32)
    shard = jnp.concatenate([shard_a, shard_b], axis=0)
    lanes = depth // nz
    for i in range(nz):
        z_out[i] = shard[:, i * lanes:(i + 1) * lanes].astype(bf16)
    z_copies = [
        push(z_out.at[p], z_in.at[i], z_send.at[i], z_recv.at[i], (2 * p + core, me))
        for i, p in enumerate(z_peers)]
    for copy in z_copies:
        copy.wait_recv()
    mine = z_out[z].astype(f32)
    for i in range(nz - 1):
        mine += z_in[i].astype(f32)
    all_in[dp] = mine.astype(bf16)
    all_copies = [
        push(all_in.at[dp], all_in.at[dp], all_send.at[i], all_recv.at[i], (p, me))
        for i, p in enumerate(dp_peers)]

    for copy in kv_copies:
        copy.wait_recv()
    for j in range(seq // 2):
        there = slice(2 * width * j, 2 * width * (j + 1))
        a, b = kv_in[2 * j], kv_in[2 * j + 1]
        dk_ref[:, there] = beside(a[:, :width], b[:, :width])
        dv_ref[:, there] = beside(a[:, width:], b[:, width:])
    for copy in all_copies:
        copy.wait_recv()
    for i in range(nz):
        tile = jnp.concatenate([all_in[2 * i], all_in[2 * i + 1]], axis=0).astype(f32)
        wg_ref[i * lanes:(i + 1) * lanes, :] = jnp.transpose(tile)
    for copy in oq_copies + kv_copies + mate_copies + line + cross + z_copies + all_copies:
        copy.wait_send()


def outward(oq, kv, grads, wt, dps):
    seq, nodes, _ = oq.shape
    depth = grads.shape[1]
    share = depth // seq
    nz = dps // 2
    rows = share // 4
    vmem = pl.BlockSpec(memory_space=pltpu.VMEM)
    dma = pltpu.SemaphoreType.DMA
    f32, bf16 = jnp.float32, jnp.bfloat16
    side = SIDE - 1
    flat = jax.ShapeDtypeStruct((nodes, depth), bf16)
    return pl.pallas_call(
        outward_kernel,
        out_shape=(flat, flat, flat, flat, jax.ShapeDtypeStruct((depth, share), f32)),
        in_specs=[vmem] * 4,
        out_specs=(vmem,) * 5,
        scratch_shapes=[
            pltpu.VMEM((seq, nodes, 128), bf16),
            pltpu.VMEM((seq, nodes, 128), bf16),
            pltpu.VMEM((nodes, depth), bf16),
            pltpu.VMEM((SIDE, SIDE, share, depth), f32),
            pltpu.VMEM((SIDE, SIDE, share // 2, depth), bf16),
            pltpu.VMEM((SIDE, SIDE, share // 2, depth), bf16),
            pltpu.VMEM((SIDE, SIDE, share // 2, depth), f32),
            pltpu.VMEM((SIDE, SIDE, share // 2, depth), bf16),
            pltpu.VMEM((2, side, SIDE, rows, depth), bf16),
            pltpu.VMEM((2, SIDE, rows, depth), bf16),
            pltpu.VMEM((2, side, rows, depth), bf16),
            pltpu.VMEM((nz, share // 2, depth // nz), bf16),
            pltpu.VMEM((max(nz - 1, 1), share // 2, depth // nz), bf16),
            pltpu.VMEM((dps, share // 2, depth // nz), bf16),
            dma((seq - 1,)), dma((seq - 1,)), dma((seq - 1,)), dma((seq - 1,)),
            dma((SIDE,)), dma((SIDE,)),
            dma((2, side)), dma((2, side)), dma((2, side)), dma((2, side)),
            dma((max(nz - 1, 1),)), dma((max(nz - 1, 1),)), dma((dps - 1,)), dma((dps - 1,)),
        ],
        compiler_params=pltpu.CompilerParams(
            collective_id=1, has_side_effects=True, vmem_limit_bytes=56 * 1024 * 1024),
        name="outward",
    )(oq, kv, grads, wt)


def on_device(queries, key_vectors, value_vectors, out_grad, proj_weight,
              cluster_order, block_cols, block_count):
    seq, dps = lax.axis_size("seq"), lax.axis_size("dp")
    qb, kv, wt = inward(
        queries[0], key_vectors[0], value_vectors[0], out_grad[0], proj_weight, seq)
    nodes = cluster_order.shape[1]
    oq, dkv = attention(
        qb.reshape(nodes, 128), kv.reshape(nodes, 128),
        cluster_order[0], block_cols[0], block_count[0])
    layer, dq, dk, dv, wg = outward(oq, dkv, out_grad[0], wt, dps)
    return layer[None], dq[None], dk[None], dv[None], wg


def solution(mesh):
    rows = P("dp", "seq", None)
    return jax.shard_map(
        on_device,
        mesh=mesh,
        in_specs=(rows, rows, rows, rows, P(None, "seq"),
                  P("dp", None), P("dp", None, None), P("dp", None)),
        out_specs=(rows, rows, rows, rows, P(None, "seq")),
        check_vma=False,
    )
```

time: 498 us -> 127 us (0.26)
  waiting for transfers between devices: 172 us -> 0 us
  local copies, waits for them, and re-layouts: 164 us -> 17.6 us
  Pallas kernels: 0 us -> 108 us
  matrix products: 83.7 us -> 0 us
  starting transfers between devices: 36.3 us -> 0 us
  blocking collectives: 14 us -> 0 us
  between operations: 14.2 us -> 0.7 us
  other arithmetic: 11.2 us -> 0 us
    psum x1 -> x0, waiting for transfers between devices: 109 us -> none  [on_device(): shard_sum = lax.psum(shard_sum, 'dp')]
    pallas_call x0 -> x3, Pallas kernels: none -> 108 us  [the longest x1 50.5 us: outward(): pl.pallas_call(outward_kernel, out_shape=(flat, flat, flat, flat, jax.Sha...]
    dot_general x43 -> x0, matrix products: 83.7 us -> none  [the longest x4 14.1 us: group_step(): jnp.einsum('rimj,rid->rmjd', grad_score, query_tile, preferred_element_ty...]
    reshape x18 -> x0, local copies, waits for them, and re-layouts: 58.8 us -> none  [the longest x4 19.9 us: group_step(): value_terms.reshape(row_blocks, list_len, tile_width)]
    gather x8 -> x0, local copies, waits for them, and re-layouts: 53.6 us -> none  [the longest x4 28.3 us: to_cluster(): return jnp.moveaxis(array[:, 0][node_order], 1, 0)]
    all_to_all x7 -> x0, starting transfers between devices: 36.2 us -> none  [the longest x1 7.58 us: on_device(): lax.all_to_all(query_h, 'seq', split_axis=1, concat_axis=0, tiled=True)]
    unnamed x4 -> x0, waiting for transfers between devices: 26.6 us -> none
    all_gather x1 -> x0, waiting for transfers between devices: 24.1 us -> none  [on_device(): full_weight = lax.all_gather(proj_weight, 'seq', axis=1, tiled=True)]
  transfers between devices with their start and end apart: 10 -> 0, of which waited for: 6 -> 0; matrix products, arithmetic and copies ran while one was open for 17% -> 0% of each run, Pallas kernels for 0% -> 0%
where the time goes in v1:
time: 127 us
  Pallas kernels  108 us (85%)
  local copies, waits for them, and re-layouts  17.6 us (14%)
    pallas_call x1, Pallas kernels, outward(): pl.pallas_call(outward_kernel, out_shape=(flat, flat, flat, flat, jax.Sha...  50.5 us
    pallas_call x1, Pallas kernels, inward(): pl.pallas_call(inward_kernel, out_shape=(jax.ShapeDtypeStruct((seq, nodes...  32.2 us
    pallas_call x1, Pallas kernels, attention(): pl.pallas_call(attention_kernel, out_shape=(jax.ShapeDtypeStruct((nodes /...  25.8 us
    unnamed x27, local copies, waits for them, and re-layouts  17.6 us

profile of v1, /device:TPU:1, one launch (start us, length us, event | category | flops | bytes accessed | tf_op | source)
XLA Modules:
  0.0 126.8 jit_solution(16426928179470387332)
XLA Ops:
  0.6 0.8 copy.13
  1.4 1.1 copy.14.w_ref
  2.5 0.0 copy-start.1
  2.5 0.9 copy-done.1
  3.4 0.0 copy-start.4
  3.4 0.9 copy-done.4
  4.4 0.0 copy-start.5
  4.4 0.9 copy-done.5
  5.3 0.0 copy-start.6
  5.3 0.9 copy-done.6
  6.3 32.2 %inward.1 = (bf16[16,128,128]{2,1,0:T(8,128)(2,1)S(1)}, bf16[16,128,128]{2,1,0:T(8,128)(2,1)S(1)}, bf16[4,4,64,1024]{3,2,1,0:T(8,128)(2,1)S(1)}) custom-call(bf16[128,1024]{1,0:T(8,128)(2,1)S(1)} %bitcast.17, bf16[128,1024]{1,0:T(8,128)(2,1)S(1)} %bitcast.18, bf16[128,1024]{1,0:T(8,128)(2,1)S(1)} %bitcast.19, bf16[128,1024]{1,0:T(8,128)(2,1)S(1)} %bitcast.14, ...), custom_call_target="tpu_custom_call" | custom-call | tf_op jit(solution)/shard_map/inward/pallas_call | solution.py:279
  38.5 0.0 copy-start
  38.5 1.3 %copy-done = bf16[4,4,64,1024]{3,2,1,0:T(8,128)(2,1)} copy-done((bf16[4,4,64,1024]{3,2,1,0:T(8,128)(2,1)}, bf16[4,4,64,1024]{3,2,1,0:T(8,128)(2,1)S(1)}, u32[]{:S(2)}) %copy-start) | copy-done | bytes 2097176
  39.8 0.0 copy-start.7
  39.8 0.7 copy-done.7
  40.5 0.0 copy-start.8
  40.5 0.7 copy-done.8
  41.2 25.8 %head_attention.1 = (bf16[16,128,128]{2,1,0:T(8,128)(2,1)S(1)}, bf16[16,128,128]{2,1,0:T(8,128)(2,1)S(1)}) custom-call(s32[32,16]{1,0:T(8,128)S(1)} %bitcast.20, s32[32]{0:T(128)S(1)} %bitcast.22, bf16[2048,128]{1,0:T(8,128)(2,1)S(1)} %bitcast.15, bf16[2048,128]{1,0:T(8,128)(2,1)S(1)} %bitcast.16, s32[16,128]{1,0:T(8,128)S(1)} %bitcast.21), custom_call_target="tpu_custom_call" | custom-call | tf_op jit(solution)/shard_map/head_attention/pallas_call | solution.py:145
  67.0 0.0 copy-start.2
  67.0 0.8 copy-done.2
  67.8 0.0 copy-start.3
  67.8 0.8 copy-done.3
  68.6 50.5 %outward.1 = (bf16[128,1024]{1,0:T(8,128)(2,1)}, bf16[128,1024]{1,0:T(8,128)(2,1)}, bf16[128,1024]{1,0:T(8,128)(2,1)}, bf16[128,1024]{1,0:T(8,128)(2,1)}, f32[1024,64]{1,0:T(8,128)}) custom-call(bf16[16,128,128]{2,1,0:T(8,128)(2,1)} %copy-done.2, bf16[16,128,128]{2,1,0:T(8,128)(2,1)} %copy-done.3, bf16[128,1024]{1,0:T(8,128)(2,1)} %bitcast.13, ...), custom_call_target="tpu_custom_call" | custom-call | tf_op jit(solution)/shard_map/outward/pallas_call | solution.py:440
  119.1 0.0 copy-start.9
  119.1 2.0 %copy.15 = f32[1024,64]{0,1:T(8,128)} copy(f32[1024,64]{1,0:T(8,128)} %get-tuple-element.29) | data formatting | bytes 524288
  121.1 1.7 %copy.20 = bf16[1,128,1024]{2,1,0:T(8,128)(2,1)} copy(bf16[1,128,1024]{2,1,0:T(8,128)(2,1)} %bitcast.26) | data formatting | bytes 524288
  122.7 1.7 %copy.21 = bf16[1,128,1024]{2,1,0:T(8,128)(2,1)} copy(bf16[1,128,1024]{2,1,0:T(8,128)(2,1)} %bitcast.25) | data formatting | bytes 524288
  124.4 1.7 %copy.22 = bf16[1,128,1024]{2,1,0:T(8,128)(2,1)} copy(bf16[1,128,1024]{2,1,0:T(8,128)(2,1)} %bitcast.24) | data formatting | bytes 524288
  126.1 0.0 copy-done.9
  126.1 0.7 copy.23
Async XLA Ops:
  2.5 1.0 copy-start.1
  3.4 0.9 copy-start.4
  4.4 0.9 copy-start.5
  5.3 0.9 copy-start.6
  38.5 1.3 %copy-start = (bf16[4,4,64,1024]{3,2,1,0:T(8,128)(2,1)}, bf16[4,4,64,1024]{3,2,1,0:T(8,128)(2,1)S(1)}, u32[]{:S(2)}) copy-start(bf16[4,4,64,1024]{3,2,1,0:T(8,128)(2,1)S(1)} %get-tuple-element.19.wt_ref) | copy-start | bytes 6291460
  39.8 0.7 copy-start.7
  40.5 0.7 copy-start.8
  67.0 0.8 copy-start.2
  67.8 0.8 copy-start.3
  119.1 7.0 %copy-start.9 = (bf16[128,1024]{1,0:T(8,128)(2,1)S(1)}, bf16[128,1024]{1,0:T(8,128)(2,1)}, u32[]{:S(2)}) copy-start(bf16[128,1024]{1,0:T(8,128)(2,1)} %get-tuple-element.23) | copy-start | bytes 786436

commit v2 on v0

v2 whole, which is shorter than its diff:
```python
import jax
import jax.numpy as jnp
from jax import lax
from jax.experimental import pallas as pl
from jax.experimental.pallas import tpu as pltpu
from jax.sharding import PartitionSpec as P

MESH = pl.DeviceIdType.MESH
SIDE = 4
BLK = 64
F32 = jnp.float32
BF16 = jnp.bfloat16
TRANS_B = (((1,), (1,)), ((), ()))


def push(src, dst, sems, at, device):
    copy = pltpu.make_async_remote_copy(
        src_ref=src, dst_ref=dst, send_sem=sems[0].at[at], recv_sem=sems[1].at[at],
        device_id=device, device_id_type=MESH)
    copy.start()
    return copy


def beside(a, b):
    return jnp.concatenate([a, b], axis=1)


def above(*parts):
    return jnp.concatenate(parts, axis=0)


def fused_kernel(
    cols_ref, count_ref, cols_vec, count_vec, order_ref, q_hbm, k_hbm, v_hbm, g_hbm, w_hbm,
    layer_ref, dq_ref, dk_ref, dv_ref, wg_ref,
    q_ref, k_ref, v_ref, g_ref, wt_ref, up_ref, slots_vec, slots_ref,
    qk_out, v_out, b_out, x_ref, v_in, b_in,
    pick_ref, unpick_ref, qq_ref, kk_ref, vv_ref, bb_ref, kt_ref, vt_ref, bt_ref,
    score_ref, soft_ref, ot_ref, term_ref, grads_ref,
    o_out, dkv_out, dq_out, o_in, dkv_in, dq_in,
    attn_ref, part_ref, mate_out, mate_in, sum_ref, half_ref, line_in, cross_out, cross_in,
    z_out, z_in, all_in,
    in_sem, slot_sem, w1_sems, w2_sems, core_sems, qk_sems, v_sems, b_sems,
    o_sems, dkv_sems, dq_sems, mate_sems, line_sems, cross_sems, z_sems, all_sems,
):
    dp, me = lax.axis_index("dp"), lax.axis_index("seq")
    seq, half_nodes, _ = v_out.shape
    dps = all_in.shape[0]
    nz = dps // 2
    nodes_dev = 2 * half_nodes
    nodes = seq * nodes_dev
    nblk = nodes // BLK
    listed = cols_ref.shape[0]
    chunks = listed // 4
    quads = nblk // 4
    depth = q_ref.shape[1]
    share = depth // seq
    y, x = me // SIDE, me % SIDE
    core, z = dp % 2, dp // 2
    mate = (dp + 1 - 2 * core, me)
    peers = [lax.rem(me + i, seq) for i in range(1, seq)]
    dp_peers = [lax.rem(dp + i, dps) for i in range(1, dps)]
    z_peers = [lax.rem(z + i, nz) for i in range(1, nz)]
    xs = [lax.rem(x + i, SIDE) for i in range(1, SIDE)]
    ys = [lax.rem(y + i, SIDE) for i in range(1, SIDE)]
    x_peers = [(dp, y * SIDE + at) for at in xs]
    y_peers = [(dp, at * SIDE + x) for at in ys]
    low128 = lax.broadcasted_iota(jnp.int32, (128, 128), 1) < BLK
    low = lax.broadcasted_iota(jnp.int32, (BLK, 128), 1) < BLK
    zero = jnp.zeros((BLK, 128), BF16)
    zero128 = jnp.zeros((128, 128), BF16)

    loads = [
        pltpu.make_async_copy(src, dst, in_sem.at[i])
        for i, (src, dst) in enumerate((
            (w_hbm, wt_ref.at[y, x]), (k_hbm, k_ref), (q_hbm, q_ref), (v_hbm, v_ref),
            (g_hbm, g_ref)))]
    for load in loads:
        load.start()
    barrier = pltpu.get_barrier_semaphore()
    for device in [(dp, p) for p in peers] + [(p, me) for p in dp_peers]:
        pl.semaphore_signal(barrier, inc=1, device_id=device, device_id_type=MESH)
    pl.semaphore_wait(barrier, seq + dps - 2)

    rows = share // 4
    start_a = pl.multiple_of(core * 2 * rows, 2 * rows)
    half_a = pl.ds(start_a, rows)
    half_b = pl.ds(pl.multiple_of(start_a + rows, rows), rows)
    loads[0].wait()
    first, second, across = [], [], []
    for i in range(SIDE - 1):
        piece = wt_ref.at[y, x, half_a]
        first.append(push(piece, piece, w1_sems, (0, i), x_peers[i]))
        piece = wt_ref.at[y, x, half_b]
        first.append(push(piece, piece, w1_sems, (1, i), y_peers[i]))

    loads[1].wait()
    loads[2].wait()
    for j in range(seq // 2):
        lanes = slice(128 * j, 128 * (j + 1))
        q, k = q_ref[:, lanes], k_ref[:, lanes]
        qk_out[2 * j] = beside(q[:, :BLK], k[:, :BLK])
        qk_out[2 * j + 1] = beside(q[:, BLK:], k[:, BLK:])
    own = pl.ds(pl.multiple_of(me * nodes_dev, nodes_dev), nodes_dev)
    x_ref[own, :128] = qk_out[me]
    qk_copies = [
        push(qk_out.at[p], x_ref.at[own, pl.ds(0, 128)], qk_sems, i, (dp, p))
        for i, p in enumerate(peers)]

    def fold(ref, out):
        for j in range(seq // 2):
            tile = ref[:, 128 * j:128 * (j + 1)]
            out[2 * j] = beside(tile[:half_nodes, :BLK], tile[half_nodes:, :BLK])
            out[2 * j + 1] = beside(tile[:half_nodes, BLK:], tile[half_nodes:, BLK:])

    def unfold(ref, out):
        for j in range(seq // 2):
            lanes = slice(128 * j, 128 * (j + 1))
            a, b = ref[2 * j], ref[2 * j + 1]
            out[:half_nodes, lanes] = beside(a[:, :BLK], b[:, :BLK])
            out[half_nodes:, lanes] = beside(a[:, BLK:], b[:, BLK:])

    loads[3].wait()
    fold(v_ref, v_out)
    v_in[me] = v_out[me]
    v_copies = [
        push(v_out.at[p], v_in.at[me], v_sems, i, (dp, p)) for i, p in enumerate(peers)]

    order = order_ref[...]
    order_col = jnp.transpose(
        above(order.astype(F32), jnp.zeros((128 - order.shape[0], 128), F32))).astype(jnp.int32)
    lane_node = lax.broadcasted_iota(jnp.int32, (128, nodes), 1)
    for i in range(nodes // 128):
        pick_ref[128 * i:128 * (i + 1), :] = (
            lane_node == order_col[:, i:i + 1]).astype(F32).astype(BF16)

    for copy in first:
        copy.wait_recv()
    for i in range(SIDE - 1):
        piece = wt_ref.at[y, :, half_a]
        second.append(push(piece, piece, w2_sems, (0, i), y_peers[i]))
        piece = wt_ref.at[:, x, half_b]
        second.append(push(piece, piece, w2_sems, (1, i), x_peers[i]))
    for i in range(SIDE - 1):
        piece = wt_ref.at[y, xs[i], half_a]
        across.append(push(piece, piece, core_sems, (0, i), mate))
        piece = wt_ref.at[ys[i], x, half_b]
        across.append(push(piece, piece, core_sems, (1, i), mate))

    order_row = jnp.concatenate([order[i:i + 1, :] for i in range(nodes // 128)], axis=1)
    row_node = lax.broadcasted_iota(jnp.int32, (128, nodes), 0)
    for j in range(nodes // 128):
        unpick_ref[128 * j:128 * (j + 1), :] = (
            row_node == order_row - 128 * j).astype(F32).astype(BF16)
    at_m = lax.broadcasted_iota(jnp.int32, (listed, nblk), 0)
    at_r = lax.broadcasted_iota(jnp.int32, (listed, nblk), 1)
    live_cols = jnp.where(at_m < count_vec[...], cols_vec[...], -1)
    place = at_r * listed + at_m
    for c in range(nblk):
        slots_vec[c:c + 1, :] = jnp.min(
            jnp.where(live_cols == c, place, nblk * listed), axis=0, keepdims=True)
    slot_copy = pltpu.make_async_copy(slots_vec, slots_ref, slot_sem)
    slot_copy.start()
    term_ref[nblk * listed] = zero

    for copy in qk_copies + v_copies:
        copy.wait_recv()
    slot_copy.wait()
    empty = jnp.zeros((half_nodes, BLK), BF16)
    for s in range(seq):
        tile = v_in[s]
        x_ref[nodes_dev * s:nodes_dev * s + half_nodes, 128:] = beside(tile[:, :BLK], empty)
        x_ref[nodes_dev * s + half_nodes:nodes_dev * (s + 1), 128:] = beside(tile[:, BLK:], empty)

    def turned(ref, i, tile):
        swap = pltpu.roll(tile, BLK, 1).astype(BF16)
        tile = tile.astype(BF16)
        ref[0, 2 * i] = jnp.where(low, tile, zero)
        ref[1, 2 * i] = jnp.where(low, zero, swap)
        ref[0, 2 * i + 1] = jnp.where(low, swap, zero)
        ref[1, 2 * i + 1] = jnp.where(low, zero, tile)

    def twice(ref, i, tile):
        ref[2 * i] = tile[:BLK]
        ref[2 * i + 1] = tile[BLK:]

    def into_cluster(i, carry):
        here = pl.ds(pl.multiple_of(i * 128, 128), 128)
        moved = jnp.dot(pick_ref[here, :], x_ref[...], preferred_element_type=F32)
        qk, v = moved[:, :128], moved[:, 128:]
        kq = pltpu.roll(qk, BLK, 1)
        twice(qq_ref, i, (jnp.where(low128, qk, kq) * 0.125).astype(BF16))
        twice(kk_ref, i, jnp.where(low128, kq, qk).astype(BF16))
        twice(vv_ref, i, (v + pltpu.roll(v, BLK, 1)).astype(BF16))
        turned(kt_ref, i, jnp.transpose(qk)[BLK:])
        turned(vt_ref, i, jnp.transpose(v)[:BLK])
        return carry

    lax.fori_loop(0, nodes // 128, into_cluster, 0)

    for i in range(SIDE - 1):
        back = SIDE - 1 - i
        second[2 * i].wait_recv()
        piece = wt_ref.at[lax.rem(y + back, SIDE), :, half_a]
        across.append(push(piece, piece, core_sems, (2, i), mate))
        second[2 * i + 1].wait_recv()
        piece = wt_ref.at[:, lax.rem(x + back, SIDE), half_b]
        across.append(push(piece, piece, core_sems, (3, i), mate))
    loads[4].wait()
    for copy in across:
        copy.wait_recv()
    up_ref[...] = jnp.dot(
        g_ref[...], wt_ref[...].reshape(depth, depth), preferred_element_type=F32).astype(BF16)
    fold(up_ref, b_out)
    b_in[me] = b_out[me]
    b_copies = [
        push(b_out.at[p], b_in.at[me], b_sems, i, (dp, p)) for i, p in enumerate(peers)]

    def diagonal(ref, i):
        blocks = []
        for j in range(4):
            tile = ref[4 * i + j]
            tile = jnp.where(low, tile, zero) if j % 2 == 0 else jnp.where(low, zero, tile)
            blocks.append(beside(tile, zero) if j < 2 else beside(zero, tile))
        return above(*blocks)

    def natural(ref, i, c):
        parts = []
        for m in range(4 * c, 4 * c + 4):
            a, b, d, e = (ref[cols_ref[m, 4 * i + j]] for j in range(4))
            parts.append(beside(jnp.where(low, a, b), jnp.where(low, d, e)))
        return above(*parts)

    def across_keys(ref, i, c):
        parts = []
        for j in range(4):
            r = 4 * i + j
            m = 4 * c
            parts.append(beside(
                ref[0, cols_ref[m, r]] + ref[1, cols_ref[m + 1, r]],
                ref[0, cols_ref[m + 2, r]] + ref[1, cols_ref[m + 3, r]]))
        return above(*parts)

    def diagonal_of(back):
        return beside(
            jnp.where(low, back[:BLK, :128], back[BLK:2 * BLK, :128]),
            jnp.where(low, back[2 * BLK:3 * BLK, 128:], back[3 * BLK:, 128:]))

    lane = lax.broadcasted_iota(jnp.int32, (1, 256), 1)

    def forward(i, carry):
        weights = diagonal(qq_ref, i)
        live = jnp.where(
            lane < 2 * BLK,
            jnp.where(lane < BLK, count_ref[4 * i], count_ref[4 * i + 1]),
            jnp.where(lane < 3 * BLK, count_ref[4 * i + 2], count_ref[4 * i + 3]))
        peak = jnp.full((8, 256), -jnp.inf, F32)
        for c in range(chunks):
            score = lax.dot_general(
                natural(kk_ref, i, c), weights, TRANS_B, preferred_element_type=F32)
            for k in range(4):
                m = 4 * c + k
                part = jnp.where(m < live, score[k * BLK:(k + 1) * BLK], -jnp.inf)
                score_ref[m * BLK:(m + 1) * BLK, :] = part
                peak = jnp.maximum(peak, jnp.max(part.reshape(8, 8, 256), axis=0))
        peak = jnp.max(peak, axis=0, keepdims=True)
        total = jnp.zeros((8, 256), F32)
        for c in range(chunks):
            here = slice(c * 256, (c + 1) * 256)
            terms = jnp.exp(score_ref[here, :] - peak)
            score_ref[here, :] = terms
            total = total + jnp.sum(terms.reshape(32, 8, 256), axis=0)
        inv = 1.0 / jnp.sum(total, axis=0, keepdims=True)
        back = jnp.zeros((256, 256), F32)
        for c in range(chunks):
            here = slice(c * 256, (c + 1) * 256)
            soft = (score_ref[here, :] * inv).astype(BF16)
            soft_ref[i, here, :] = soft
            back = back + jnp.dot(across_keys(vt_ref, i, c), soft, preferred_element_type=F32)
        ot_ref[:, pl.ds(pl.multiple_of(i * 256, 256), 256)] = diagonal_of(back).astype(BF16)
        return carry

    lax.fori_loop(0, quads, forward, 0)

    def outputs_back(j, carry):
        here = pl.ds(pl.multiple_of(j * 128, 128), 128)
        moved = lax.dot_general(
            unpick_ref[here, :], ot_ref[...], TRANS_B, preferred_element_type=F32).astype(BF16)
        o_out[j] = beside(moved[:half_nodes], moved[half_nodes:])
        return carry

    lax.fori_loop(0, seq, outputs_back, 0)
    o_in[me] = o_out[me]
    o_copies = [
        push(o_out.at[p], o_in.at[me], o_sems, i, (dp, p)) for i, p in enumerate(peers)]

    for copy in b_copies:
        copy.wait_recv()
    for s in range(seq):
        tile = b_in[s]
        x_ref[nodes_dev * s:nodes_dev * s + half_nodes, 128:] = beside(
            tile[:, :BLK], tile[:, :BLK])
        x_ref[nodes_dev * s + half_nodes:nodes_dev * (s + 1), 128:] = beside(
            tile[:, BLK:], tile[:, BLK:])

    def upstream_into_cluster(i, carry):
        here = pl.ds(pl.multiple_of(i * 128, 128), 128)
        moved = jnp.dot(pick_ref[here, :], x_ref[:, 128:], preferred_element_type=F32)
        twice(bb_ref, i, moved.astype(BF16))
        bt_ref[:, here] = jnp.transpose(moved)[:BLK]
        return carry

    lax.fori_loop(0, nodes // 128, upstream_into_cluster, 0)

    def backward(i, carry):
        there = pl.ds(pl.multiple_of(i * 256, 256), 256)
        delta = jnp.sum(ot_ref[:, there].astype(F32) * bt_ref[:, there], axis=0, keepdims=True)
        weights = diagonal(bb_ref, i)
        pair_weights = []
        for j in (0, 2):
            q1, q2, b1, b2 = (ref[4 * i + j + k] for ref in (qq_ref, bb_ref) for k in (0, 1))
            pair_weights.append(above(
                beside(jnp.where(low, zero, b1), zero), beside(zero, jnp.where(low, zero, b2)),
                beside(jnp.where(low, q1, zero), zero), beside(zero, jnp.where(low, q2, zero))))
        back = jnp.zeros((256, 256), F32)
        for c in range(chunks):
            here = slice(c * 256, (c + 1) * 256)
            grad = lax.dot_general(
                natural(vv_ref, i, c), weights, TRANS_B, preferred_element_type=F32)
            soft = soft_ref[i, here, :]
            grad = (soft.astype(F32) * (grad - delta)).astype(BF16)
            for j in range(2):
                lanes = slice(128 * j, 128 * (j + 1))
                terms = jnp.dot(
                    beside(soft[:, lanes], grad[:, lanes]), pair_weights[j],
                    preferred_element_type=F32).astype(BF16)
                for k in range(4):
                    m = 4 * c + k
                    slot = (4 * i + 2 * j) * listed + m
                    term_ref[slot] = terms[k * BLK:(k + 1) * BLK, :128]
                    term_ref[slot + listed] = terms[k * BLK:(k + 1) * BLK, 128:]
            back = back + jnp.dot(across_keys(kt_ref, i, c), grad, preferred_element_type=F32)
        grad_q = jnp.transpose(diagonal_of(back) * 0.125).astype(BF16)
        grads_ref[there, 128:] = beside(grad_q, jnp.zeros_like(grad_q))
        return carry

    lax.fori_loop(0, 3, backward, 0)

    for copy in o_copies:
        copy.wait_recv()
    unfold(o_in, attn_ref)
    keep = pl.ds(pl.multiple_of(core * (share // 2), share // 2), share // 2)
    give = pl.ds(pl.multiple_of((1 - core) * (share // 2), share // 2), share // 2)
    mate_copies = []
    for c in range(SIDE):
        part_ref[...] = lax.dot_general(
            g_ref[:, c * SIDE * share:(c + 1) * SIDE * share], attn_ref[...],
            (((0,), (0,)), ((), ())), preferred_element_type=F32).reshape(SIDE, share, depth)
        mate_out[c] = part_ref[:, give, :].astype(BF16)
        sum_ref[c] = part_ref[:, keep, :]
        mate_copies.append(push(mate_out.at[c], mate_in.at[c], mate_sems, c, mate))
    layer_ref[...] = lax.dot_general(
        attn_ref[...], wt_ref[...].reshape(depth, depth), TRANS_B,
        preferred_element_type=F32).astype(BF16)
    for c in range(SIDE):
        mate_copies[c].wait_recv()
        total = sum_ref[c] + mate_in[c].astype(F32)
        sum_ref[c] = total
        half_ref[c] = total.astype(BF16)
    line = []
    for i in range(SIDE - 1):
        line.append(push(
            half_ref.at[:, xs[i], pl.ds(0, rows)], line_in.at[0, i], line_sems, (0, i),
            x_peers[i]))
        line.append(push(
            half_ref.at[ys[i], :, pl.ds(rows, rows)], line_in.at[1, i], line_sems, (1, i),
            y_peers[i]))

    lax.fori_loop(3, quads, backward, 0)

    for copy in line:
        copy.wait_recv()
    sum_a = sum_ref[:, pl.ds(x, 1), :rows, :].reshape(SIDE, rows, depth)
    sum_b = sum_ref[pl.ds(y, 1), :, rows:, :].reshape(SIDE, rows, depth)
    for i in range(SIDE - 1):
        sum_a += line_in[0, i].astype(F32)
        sum_b += line_in[1, i].astype(F32)
    cross_out[0] = sum_a.astype(BF16)
    cross_out[1] = sum_b.astype(BF16)
    cross = []
    for i in range(SIDE - 1):
        cross.append(push(
            cross_out.at[0, ys[i]], cross_in.at[0, i], cross_sems, (0, i), y_peers[i]))
        cross.append(push(
            cross_out.at[1, xs[i]], cross_in.at[1, i], cross_sems, (1, i), x_peers[i]))

    def gather_terms(c, carry):
        total = term_ref[slots_ref[c, 0]].astype(F32)
        for r in range(1, nblk):
            total = total + term_ref[slots_ref[c, r]].astype(F32)
        grads_ref[pl.ds(pl.multiple_of(c * BLK, BLK), BLK), :128] = total.astype(BF16)
        return carry

    lax.fori_loop(0, nblk, gather_terms, 0)

    for copy in cross:
        copy.wait_recv()
    shard_a = cross_out[0, y].astype(F32)
    shard_b = cross_out[1, x].astype(F32)
    for i in range(SIDE - 1):
        shard_a += cross_in[0, i].astype(F32)
        shard_b += cross_in[1, i].astype(F32)
    shard = above(shard_a, shard_b)
    lanes = depth // nz
    for i in range(nz):
        z_out[i] = shard[:, i * lanes:(i + 1) * lanes].astype(BF16)
    z_copies = [
        push(z_out.at[p], z_in.at[i], z_sems, i, (2 * p + core, me))
        for i, p in enumerate(z_peers)]

    def grads_back(j, carry):
        here = pl.ds(pl.multiple_of(j * 128, 128), 128)
        moved = jnp.dot(
            unpick_ref[here, :], grads_ref[...], preferred_element_type=F32).astype(BF16)
        dkv_out[j] = moved[:, :128]
        dq_out[j] = beside(moved[:half_nodes, 128:128 + BLK], moved[half_nodes:, 128:128 + BLK])
        return carry

    lax.fori_loop(0, seq, grads_back, 0)
    dkv_in[me] = dkv_out[me]
    dkv_copies = [
        push(dkv_out.at[p], dkv_in.at[me], dkv_sems, i, (dp, p)) for i, p in enumerate(peers)]
    dq_in[me] = dq_out[me]
    dq_copies = [
        push(dq_out.at[p], dq_in.at[me], dq_sems, i, (dp, p)) for i, p in enumerate(peers)]

    for copy in z_copies:
        copy.wait_recv()
    mine = z_out[z].astype(F32)
    for i in range(nz - 1):
        mine += z_in[i].astype(F32)
    all_in[dp] = mine.astype(BF16)
    all_copies = [
        push(all_in.at[dp], all_in.at[dp], all_sems, i, (p, me))
        for i, p in enumerate(dp_peers)]

    for copy in dkv_copies:
        copy.wait_recv()
    for j in range(seq // 2):
        there = slice(128 * j, 128 * (j + 1))
        a, b = dkv_in[2 * j], dkv_in[2 * j + 1]
        dk_ref[:, there] = beside(a[:, :BLK], b[:, :BLK])
        dv_ref[:, there] = beside(a[:, BLK:], b[:, BLK:])
    for copy in dq_copies:
        copy.wait_recv()
    unfold(dq_in, dq_ref)
    for copy in all_copies:
        copy.wait_recv()
    for i in range(dps):
        wg_ref[i % 2 * (share // 2):(i % 2 + 1) * (share // 2),
               i // 2 * lanes:(i // 2 + 1) * lanes] = all_in[i].astype(F32)
    for copy in (first + second + across + qk_copies + v_copies + b_copies + o_copies
                 + mate_copies + line + cross + z_copies + dkv_copies + dq_copies + all_copies):
        copy.wait_send()


def fused(q, k, v, g, wt, order, cols, count, seq, dps):
    nodes_dev, depth = q.shape
    nodes = seq * nodes_dev
    listed, nblk = cols.shape
    share = depth // seq
    nz = dps // 2
    rows = share // 4
    side = SIDE - 1
    smem = pl.BlockSpec(memory_space=pltpu.SMEM)
    vmem = pl.BlockSpec(memory_space=pltpu.VMEM)
    hbm = pl.BlockSpec(memory_space=pl.ANY)

    def dma(*shape):
        return (pltpu.SemaphoreType.DMA(shape), pltpu.SemaphoreType.DMA(shape))

    flat = jax.ShapeDtypeStruct((nodes_dev, depth), BF16)
    big = pltpu.VMEM((nodes_dev, depth), BF16)
    per_head = pltpu.VMEM((seq, nodes_dev, 128), BF16)
    folded = pltpu.VMEM((seq, nodes_dev // 2, 128), BF16)
    blocks = pltpu.VMEM((nblk, BLK, 128), BF16)
    turned = pltpu.VMEM((2, nblk, BLK, 128), BF16)
    pick = pltpu.VMEM((nodes, nodes), BF16)
    half = pltpu.VMEM((SIDE, SIDE, share // 2, depth), BF16)
    few = max(nz - 1, 1)
    return pl.pallas_call(
        fused_kernel,
        out_shape=(flat, flat, flat, flat, jax.ShapeDtypeStruct((share, depth), F32)),
        in_specs=[smem, smem, vmem, vmem, vmem] + [hbm] * 5,
        out_specs=(vmem,) * 5,
        scratch_shapes=[
            big, big, big, big,
            pltpu.VMEM((SIDE, SIDE, share, depth), BF16),
            big,
            pltpu.VMEM((nblk, nblk), jnp.int32), pltpu.SMEM((nblk, nblk), jnp.int32),
            per_head, folded, folded, pltpu.VMEM((nodes, 256), BF16), folded, folded,
            pick, pick, blocks, blocks, blocks, blocks, turned, turned,
            pltpu.VMEM((BLK, nodes), F32),
            pltpu.VMEM((listed * BLK, 256), F32),
            pltpu.VMEM((nblk // 4, listed * BLK, 256), BF16),
            pltpu.VMEM((BLK, nodes), BF16),
            pltpu.VMEM((nblk * listed + 1, BLK, 128), BF16),
            pltpu.VMEM((nodes, 256), BF16),
            folded, per_head, folded, folded, per_head, folded,
            big,
            pltpu.VMEM((SIDE, share, depth), F32),
            half, half, pltpu.VMEM((SIDE, SIDE, share // 2, depth), F32), half,
            pltpu.VMEM((2, side, SIDE, rows, depth), BF16),
            pltpu.VMEM((2, SIDE, rows, depth), BF16),
            pltpu.VMEM((2, side, rows, depth), BF16),
            pltpu.VMEM((nz, share // 2, depth // nz), BF16),
            pltpu.VMEM((few, share // 2, depth // nz), BF16),
            pltpu.VMEM((dps, share // 2, depth // nz), BF16),
            pltpu.SemaphoreType.DMA((5,)), pltpu.SemaphoreType.DMA,
            dma(2, side), dma(2, side), dma(4, side), dma(seq - 1), dma(seq - 1), dma(seq - 1),
            dma(seq - 1), dma(seq - 1), dma(seq - 1), dma(SIDE), dma(2, side), dma(2, side),
            dma(few), dma(dps - 1),
        ],
        compiler_params=pltpu.CompilerParams(
            collective_id=0, has_side_effects=True, vmem_limit_bytes=62 * 1024 * 1024),
        name="layer",
    )(cols, count, cols, count.reshape(1, nblk), order.reshape(nodes // 128, 128), q, k, v, g, wt)


def finish_kernel(*refs):
    copies = [
        pltpu.make_async_copy(src, dst, refs[-1].at[i])
        for i, (src, dst) in enumerate(zip(refs[:5], refs[5:10]))]
    for copy in copies:
        copy.start()
    for copy in copies:
        copy.wait()


def finish(arrays):
    hbm = pl.BlockSpec(memory_space=pl.ANY)
    return pl.pallas_call(
        finish_kernel,
        out_shape=tuple(jax.ShapeDtypeStruct(a.shape, a.dtype) for a in arrays),
        in_specs=[hbm] * 5,
        out_specs=(hbm,) * 5,
        scratch_shapes=[pltpu.SemaphoreType.DMA((5,))],
        name="finish",
    )(*arrays)


def on_device(queries, key_vectors, value_vectors, out_grad, proj_weight,
              cluster_order, block_cols, block_count):
    seq, dps = lax.axis_size("seq"), lax.axis_size("dp")
    layer, dq, dk, dv, wg = finish(fused(
        queries[0], key_vectors[0], value_vectors[0], out_grad[0], proj_weight.T,
        cluster_order[0], block_cols[0].T, block_count[0], seq, dps))
    return layer[None], dq[None], dk[None], dv[None], wg.T


def solution(mesh):
    rows = P("dp", "seq", None)
    return jax.shard_map(
        on_device,
        mesh=mesh,
        in_specs=(rows, rows, rows, rows, P(None, "seq"),
                  P("dp", None), P("dp", None, None), P("dp", None)),
        out_specs=(rows, rows, rows, rows, P(None, "seq")),
        check_vma=False,
    )
```

time: 498 us -> 136 us (0.27)
  waiting for transfers between devices: 172 us -> 0 us
  local copies, waits for them, and re-layouts: 164 us -> 0 us
  Pallas kernels: 0 us -> 134 us
  matrix products: 83.7 us -> 0 us
  starting transfers between devices: 36.3 us -> 0 us
  blocking collectives: 14 us -> 0 us
  between operations: 14.2 us -> 0.8 us
  other arithmetic: 11.2 us -> 0 us
    pallas_call x0 -> x2, Pallas kernels: none -> 134 us  [the longest x1 93.4 us: fused(): pl.pallas_call(fused_kernel, out_shape=(flat, flat, flat, flat, jax.Shape...]
    psum x1 -> x0, waiting for transfers between devices: 109 us -> none  [on_device(): shard_sum = lax.psum(shard_sum, 'dp')]
    dot_general x43 -> x0, matrix products: 83.7 us -> none  [the longest x4 14.1 us: group_step(): jnp.einsum('rimj,rid->rmjd', grad_score, query_tile, preferred_element_ty...]
    reshape x18 -> x0, local copies, waits for them, and re-layouts: 58.8 us -> none  [the longest x4 19.9 us: group_step(): value_terms.reshape(row_blocks, list_len, tile_width)]
    gather x8 -> x0, local copies, waits for them, and re-layouts: 53.6 us -> none  [the longest x4 28.3 us: to_cluster(): return jnp.moveaxis(array[:, 0][node_order], 1, 0)]
    all_to_all x7 -> x0, starting transfers between devices: 36.2 us -> none  [the longest x1 7.58 us: on_device(): lax.all_to_all(query_h, 'seq', split_axis=1, concat_axis=0, tiled=True)]
    unnamed x41 -> x0, local copies, waits for them, and re-layouts: 29.3 us -> none
    unnamed x4 -> x0, waiting for transfers between devices: 26.6 us -> none
  transfers between devices with their start and end apart: 10 -> 0, of which waited for: 6 -> 0; matrix products, arithmetic and copies ran while one was open for 17% -> 0% of each run, Pallas kernels for 0% -> 0%
where the time goes in v2:
time: 136 us; the launch traced here: 135 us
  Pallas kernels  134 us (99%)
    pallas_call x1, Pallas kernels, fused(): pl.pallas_call(fused_kernel, out_shape=(flat, flat, flat, flat, jax.Shape...  93.4 us
    pallas_call x1, Pallas kernels, finish(): pl.pallas_call(finish_kernel, out_shape=tuple((jax.ShapeDtypeStruct(a.sha...  40.9 us

profile of v2, /device:TPU:1, one launch (start us, length us, event | category | flops | bytes accessed | tf_op | source)
XLA Modules:
  0.0 135.0 jit_solution(6600707256983605407)
XLA Ops:
  0.6 93.4 %layer.1 = (bf16[128,1024]{1,0:T(8,128)(2,1)}, bf16[128,1024]{1,0:T(8,128)(2,1)}, bf16[128,1024]{1,0:T(8,128)(2,1)}, bf16[128,1024]{1,0:T(8,128)(2,1)}, f32[64,1024]{1,0:T(8,128)}) custom-call(s32[16,32]{1,0:T(8,128)} %bitcast.20, s32[32]{0:T(128)} %bitcast.23, s32[16,32]{1,0:T(8,128)} %bitcast.21, s32[1,32]{1,0:T(1,128)} %count_vec.1, s32[16,128]{1,0:T(8,128)} %bitcast.22, ...), custom_call_target="tpu_custom_call" | custom-call | tf_op jit(solution)/shard_map/layer/pallas_call | solution.py:490
  94.0 40.9 %finish.1 = (bf16[128,1024]{1,0:T(8,128)(2,1)}, bf16[128,1024]{1,0:T(8,128)(2,1)}, bf16[128,1024]{1,0:T(8,128)(2,1)}, bf16[128,1024]{1,0:T(8,128)(2,1)}, f32[64,1024]{1,0:T(8,128)}) custom-call(bf16[128,1024]{1,0:T(8,128)(2,1)} %get-tuple-element.15.refs_0_, bf16[128,1024]{1,0:T(8,128)(2,1)} %get-tuple-element.16.refs_1_, ...), custom_call_target="tpu_custom_call" | custom-call | tf_op jit(solution)/shard_map/finish/pallas_call | solution.py:541

commit v3 on v2

--- a/solution.py
+++ b/solution.py
@@ -7,6 +7,10 @@
 
 MESH = pl.DeviceIdType.MESH
 SIDE = 4
+STEPS = (
+    (2, 2), (3, 2), (2, 3), (1, 2), (2, 1), (2, 0), (0, 2), (3, 1), (1, 3), (3, 3), (1, 1),
+    (3, 0), (1, 0), (0, 3), (0, 1))
+TILE = 512
 BLK = 64
 F32 = jnp.float32
 BF16 = jnp.bfloat16
@@ -32,10 +36,10 @@
 def fused_kernel(
     cols_ref, count_ref, cols_vec, count_vec, order_ref, q_hbm, k_hbm, v_hbm, g_hbm, w_hbm,
     layer_ref, dq_ref, dk_ref, dv_ref, wg_ref,
-    q_ref, k_ref, v_ref, g_ref, wt_ref, up_ref, slots_vec, slots_ref,
+    q_ref, k_ref, v_ref, g_ref, gt_ref, wt_ref, up_ref, slots_vec, slots_ref,
     qk_out, v_out, b_out, x_ref, v_in, b_in,
     pick_ref, unpick_ref, qq_ref, kk_ref, vv_ref, bb_ref, kt_ref, vt_ref, bt_ref,
-    score_ref, soft_ref, ot_ref, term_ref, grads_ref,
+    score_ref, soft_ref, ot_ref, on_ref, term_ref, grads_ref,
     o_out, dkv_out, dq_out, o_in, dkv_in, dq_in,
     attn_ref, part_ref, mate_out, mate_in, sum_ref, half_ref, line_in, cross_out, cross_in,
     z_out, z_in, all_in,
@@ -44,8 +48,7 @@
 ):
     dp, me = lax.axis_index("dp"), lax.axis_index("seq")
     seq, half_nodes, _ = v_out.shape
-    dps = all_in.shape[0]
-    nz = dps // 2
+    nz = all_in.shape[1]
     nodes_dev = 2 * half_nodes
     nodes = seq * nodes_dev
     nblk = nodes // BLK
@@ -57,8 +60,7 @@
     y, x = me // SIDE, me % SIDE
     core, z = dp % 2, dp // 2
     mate = (dp + 1 - 2 * core, me)
-    peers = [lax.rem(me + i, seq) for i in range(1, seq)]
-    dp_peers = [lax.rem(dp + i, dps) for i in range(1, dps)]
+    peers = [lax.rem(y + dy, SIDE) * SIDE + lax.rem(x + dx, SIDE) for dy, dx in STEPS]
     z_peers = [lax.rem(z + i, nz) for i in range(1, nz)]
     xs = [lax.rem(x + i, SIDE) for i in range(1, SIDE)]
     ys = [lax.rem(y + i, SIDE) for i in range(1, SIDE)]
@@ -77,9 +79,10 @@
     for load in loads:
         load.start()
     barrier = pltpu.get_barrier_semaphore()
-    for device in [(dp, p) for p in peers] + [(p, me) for p in dp_peers]:
+    greeted = [(dp, p) for p in peers] + [(2 * p + core, me) for p in z_peers] + [mate]
+    for device in greeted:
         pl.semaphore_signal(barrier, inc=1, device_id=device, device_id_type=MESH)
-    pl.semaphore_wait(barrier, seq + dps - 2)
+    pl.semaphore_wait(barrier, len(greeted))
 
     rows = share // 4
     start_a = pl.multiple_of(core * 2 * rows, 2 * rows)
@@ -135,6 +138,7 @@
 
     for copy in first:
         copy.wait_recv()
+    loads[4].wait()
     for i in range(SIDE - 1):
         piece = wt_ref.at[y, :, half_a]
         second.append(push(piece, piece, w2_sems, (0, i), y_peers[i]))
@@ -146,6 +150,8 @@
         piece = wt_ref.at[ys[i], x, half_b]
         across.append(push(piece, piece, core_sems, (1, i), mate))
 
+    for i in range(depth // 128):
+        gt_ref[128 * i:128 * (i + 1), :] = jnp.transpose(g_ref[:, 128 * i:128 * (i + 1)])
     order_row = jnp.concatenate([order[i:i + 1, :] for i in range(nodes // 128)], axis=1)
     row_node = lax.broadcasted_iota(jnp.int32, (128, nodes), 0)
     for j in range(nodes // 128):
@@ -183,19 +189,22 @@
         ref[2 * i] = tile[:BLK]
         ref[2 * i + 1] = tile[BLK:]
 
-    def into_cluster(i, carry):
-        here = pl.ds(pl.multiple_of(i * 128, 128), 128)
-        moved = jnp.dot(pick_ref[here, :], x_ref[...], preferred_element_type=F32)
-        qk, v = moved[:, :128], moved[:, 128:]
-        kq = pltpu.roll(qk, BLK, 1)
-        twice(qq_ref, i, (jnp.where(low128, qk, kq) * 0.125).astype(BF16))
-        twice(kk_ref, i, jnp.where(low128, kq, qk).astype(BF16))
-        twice(vv_ref, i, (v + pltpu.roll(v, BLK, 1)).astype(BF16))
-        turned(kt_ref, i, jnp.transpose(qk)[BLK:])
-        turned(vt_ref, i, jnp.transpose(v)[:BLK])
+    def into_cluster(t, carry):
+        here = pl.ds(pl.multiple_of(t * TILE, TILE), TILE)
+        tile = jnp.dot(pick_ref[here, :], x_ref[...], preferred_element_type=F32)
+        for k in range(TILE // 128):
+            moved = tile[128 * k:128 * (k + 1)]
+            i = t * (TILE // 128) + k
+            qk, v = moved[:, :128], moved[:, 128:]
+            kq = pltpu.roll(qk, BLK, 1)
+            twice(qq_ref, i, (jnp.where(low128, qk, kq) * 0.125).astype(BF16))
+            twice(kk_ref, i, jnp.where(low128, kq, qk).astype(BF16))
+            twice(vv_ref, i, (v + pltpu.roll(v, BLK, 1)).astype(BF16))
+            turned(kt_ref, i, jnp.transpose(qk)[BLK:])
+            turned(vt_ref, i, jnp.transpose(v)[:BLK])
         return carry
 
-    lax.fori_loop(0, nodes // 128, into_cluster, 0)
+    lax.fori_loop(0, nodes // TILE, into_cluster, 0)
 
     for i in range(SIDE - 1):
         back = SIDE - 1 - i
@@ -205,7 +214,6 @@
         second[2 * i + 1].wait_recv()
         piece = wt_ref.at[:, lax.rem(x + back, SIDE), half_b]
         across.append(push(piece, piece, core_sems, (3, i), mate))
-    loads[4].wait()
     for copy in across:
         copy.wait_recv()
     up_ref[...] = jnp.dot(
@@ -276,19 +284,30 @@
             soft = (score_ref[here, :] * inv).astype(BF16)
             soft_ref[i, here, :] = soft
             back = back + jnp.dot(across_keys(vt_ref, i, c), soft, preferred_element_type=F32)
-        ot_ref[:, pl.ds(pl.multiple_of(i * 256, 256), 256)] = diagonal_of(back).astype(BF16)
+        there = pl.ds(pl.multiple_of(i * 256, 256), 256)
+        out = diagonal_of(back)
+        ot_ref[:, there] = out.astype(BF16)
+        out = jnp.transpose(out).astype(BF16)
+        on_ref[there, :] = beside(out, jnp.zeros_like(out))
         return carry
 
     lax.fori_loop(0, quads, forward, 0)
 
-    def outputs_back(j, carry):
-        here = pl.ds(pl.multiple_of(j * 128, 128), 128)
-        moved = lax.dot_general(
-            unpick_ref[here, :], ot_ref[...], TRANS_B, preferred_element_type=F32).astype(BF16)
-        o_out[j] = beside(moved[:half_nodes], moved[half_nodes:])
-        return carry
-
-    lax.fori_loop(0, seq, outputs_back, 0)
+    def fold_rows(tile):
+        return beside(tile[:half_nodes, :BLK], tile[half_nodes:, :BLK])
+
+    def back_to_nodes(ref, lanes, out, pack):
+        def step(t, carry):
+            here = pl.ds(pl.multiple_of(t * TILE, TILE), TILE)
+            tile = jnp.dot(
+                unpick_ref[here, :], ref[:, lanes], preferred_element_type=F32).astype(BF16)
+            for k in range(TILE // 128):
+                out[t * (TILE // 128) + k] = pack(tile[128 * k:128 * (k + 1)])
+            return carry
+
+        lax.fori_loop(0, nodes // TILE, step, 0)
+
+    back_to_nodes(on_ref, slice(0, 128), o_out, fold_rows)
     o_in[me] = o_out[me]
     o_copies = [
         push(o_out.at[p], o_in.at[me], o_sems, i, (dp, p)) for i, p in enumerate(peers)]
@@ -302,14 +321,17 @@
         x_ref[nodes_dev * s + half_nodes:nodes_dev * (s + 1), 128:] = beside(
             tile[:, BLK:], tile[:, BLK:])
 
-    def upstream_into_cluster(i, carry):
-        here = pl.ds(pl.multiple_of(i * 128, 128), 128)
-        moved = jnp.dot(pick_ref[here, :], x_ref[:, 128:], preferred_element_type=F32)
-        twice(bb_ref, i, moved.astype(BF16))
-        bt_ref[:, here] = jnp.transpose(moved)[:BLK]
+    def upstream_into_cluster(t, carry):
+        here = pl.ds(pl.multiple_of(t * TILE, TILE), TILE)
+        tile = jnp.dot(pick_ref[here, :], x_ref[:, 128:], preferred_element_type=F32)
+        for k in range(TILE // 128):
+            moved = tile[128 * k:128 * (k + 1)]
+            i = t * (TILE // 128) + k
+            twice(bb_ref, i, moved.astype(BF16))
+            bt_ref[:, pl.ds(pl.multiple_of(i * 128, 128), 128)] = jnp.transpose(moved)[:BLK]
         return carry
 
-    lax.fori_loop(0, nodes // 128, upstream_into_cluster, 0)
+    lax.fori_loop(0, nodes // TILE, upstream_into_cluster, 0)
 
     def backward(i, carry):
         there = pl.ds(pl.multiple_of(i * 256, 256), 256)
@@ -343,41 +365,61 @@
         grads_ref[there, 128:] = beside(grad_q, jnp.zeros_like(grad_q))
         return carry
 
-    lax.fori_loop(0, 3, backward, 0)
+    lax.fori_loop(0, 4, backward, 0)
 
     for copy in o_copies:
         copy.wait_recv()
     unfold(o_in, attn_ref)
     keep = pl.ds(pl.multiple_of(core * (share // 2), share // 2), share // 2)
     give = pl.ds(pl.multiple_of((1 - core) * (share // 2), share // 2), share // 2)
+    order_y = ys + [y]
     mate_copies = []
-    for c in range(SIDE):
-        part_ref[...] = lax.dot_general(
-            g_ref[:, c * SIDE * share:(c + 1) * SIDE * share], attn_ref[...],
-            (((0,), (0,)), ((), ())), preferred_element_type=F32).reshape(SIDE, share, depth)
-        mate_out[c] = part_ref[:, give, :].astype(BF16)
-        sum_ref[c] = part_ref[:, keep, :]
-        mate_copies.append(push(mate_out.at[c], mate_in.at[c], mate_sems, c, mate))
+    for c, at in enumerate(order_y):
+        there = pl.ds(pl.multiple_of(at * (SIDE * share), SIDE * share), SIDE * share)
+        part_ref[...] = jnp.dot(
+            gt_ref[there, :], attn_ref[...], preferred_element_type=F32).reshape(
+                SIDE, share, depth)
+        mate_out[at] = part_ref[:, give, :].astype(BF16)
+        sum_ref[at] = part_ref[:, keep, :]
+        mate_copies.append(push(mate_out.at[at], mate_in.at[at], mate_sems, c, mate))
+
+    lax.fori_loop(4, 5, backward, 0)
+
+    line_a, line_b = [], []
+    for c, at in enumerate(order_y):
+        mate_copies[c].wait_recv()
+        total = sum_ref[at] + mate_in[at].astype(F32)
+        sum_ref[at] = total
+        half_ref[at] = total.astype(BF16)
+        for i in range(SIDE - 1):
+            line_a.append(push(
+                half_ref.at[at, xs[i], pl.ds(0, rows)], line_in.at[0, i, at], line_sems, (c, i),
+                x_peers[i]))
+        if c < SIDE - 1:
+            line_b.append(push(
+                half_ref.at[at, :, pl.ds(rows, rows)], line_in.at[1, c], line_sems, (SIDE, c),
+                y_peers[c]))
     layer_ref[...] = lax.dot_general(
         attn_ref[...], wt_ref[...].reshape(depth, depth), TRANS_B,
         preferred_element_type=F32).astype(BF16)
-    for c in range(SIDE):
-        mate_copies[c].wait_recv()
-        total = sum_ref[c] + mate_in[c].astype(F32)
-        sum_ref[c] = total
-        half_ref[c] = total.astype(BF16)
-    line = []
-    for i in range(SIDE - 1):
-        line.append(push(
-            half_ref.at[:, xs[i], pl.ds(0, rows)], line_in.at[0, i], line_sems, (0, i),
-            x_peers[i]))
-        line.append(push(
-            half_ref.at[ys[i], :, pl.ds(rows, rows)], line_in.at[1, i], line_sems, (1, i),
-            y_peers[i]))
-
-    lax.fori_loop(3, quads, backward, 0)
-
-    for copy in line:
+
+    lax.fori_loop(5, quads, backward, 0)
+
+    back_to_nodes(grads_ref, slice(128, 256), dq_out, fold_rows)
+    dq_in[me] = dq_out[me]
+    dq_copies = [
+        push(dq_out.at[p], dq_in.at[me], dq_sems, i, (dp, p)) for i, p in enumerate(peers)]
+
+    def gather_terms(c, carry):
+        total = term_ref[slots_ref[c, 0]].astype(F32)
+        for r in range(1, nblk):
+            total = total + term_ref[slots_ref[c, r]].astype(F32)
+        grads_ref[pl.ds(pl.multiple_of(c * BLK, BLK), BLK), :128] = total.astype(BF16)
+        return carry
+
+    lax.fori_loop(0, nblk, gather_terms, 0)
+
+    for copy in line_a + line_b:
         copy.wait_recv()
     sum_a = sum_ref[:, pl.ds(x, 1), :rows, :].reshape(SIDE, rows, depth)
     sum_b = sum_ref[pl.ds(y, 1), :, rows:, :].reshape(SIDE, rows, depth)
@@ -393,14 +435,10 @@
         cross.append(push(
             cross_out.at[1, xs[i]], cross_in.at[1, i], cross_sems, (1, i), x_peers[i]))
 
-    def gather_terms(c, carry):
-        total = term_ref[slots_ref[c, 0]].astype(F32)
-        for r in range(1, nblk):
-            total = total + term_ref[slots_ref[c, r]].astype(F32)
-        grads_ref[pl.ds(pl.multiple_of(c * BLK, BLK), BLK), :128] = total.astype(BF16)
-        return carry
-
-    lax.fori_loop(0, nblk, gather_terms, 0)
+    back_to_nodes(grads_ref, slice(0, 128), dkv_out, lambda tile: tile)
+    dkv_in[me] = dkv_out[me]
+    dkv_copies = [
+        push(dkv_out.at[p], dkv_in.at[me], dkv_sems, i, (dp, p)) for i, p in enumerate(peers)]
 
     for copy in cross:
         copy.wait_recv()
@@ -416,32 +454,18 @@
     z_copies = [
         push(z_out.at[p], z_in.at[i], z_sems, i, (2 * p + core, me))
         for i, p in enumerate(z_peers)]
-
-    def grads_back(j, carry):
-        here = pl.ds(pl.multiple_of(j * 128, 128), 128)
-        moved = jnp.dot(
-            unpick_ref[here, :], grads_ref[...], preferred_element_type=F32).astype(BF16)
-        dkv_out[j] = moved[:, :128]
-        dq_out[j] = beside(moved[:half_nodes, 128:128 + BLK], moved[half_nodes:, 128:128 + BLK])
-        return carry
-
-    lax.fori_loop(0, seq, grads_back, 0)
-    dkv_in[me] = dkv_out[me]
-    dkv_copies = [
-        push(dkv_out.at[p], dkv_in.at[me], dkv_sems, i, (dp, p)) for i, p in enumerate(peers)]
-    dq_in[me] = dq_out[me]
-    dq_copies = [
-        push(dq_out.at[p], dq_in.at[me], dq_sems, i, (dp, p)) for i, p in enumerate(peers)]
-
+    for copy in dq_copies:
+        copy.wait_recv()
+    unfold(dq_in, dq_ref)
     for copy in z_copies:
         copy.wait_recv()
     mine = z_out[z].astype(F32)
     for i in range(nz - 1):
         mine += z_in[i].astype(F32)
-    all_in[dp] = mine.astype(BF16)
+    all_in[core, z] = mine.astype(BF16)
     all_copies = [
-        push(all_in.at[dp], all_in.at[dp], all_sems, i, (p, me))
-        for i, p in enumerate(dp_peers)]
+        push(all_in.at[core, z], all_in.at[core, z], all_sems, i, (2 * p + core, me))
+        for i, p in enumerate(z_peers)]
 
     for copy in dkv_copies:
         copy.wait_recv()
@@ -450,16 +474,17 @@
         a, b = dkv_in[2 * j], dkv_in[2 * j + 1]
         dk_ref[:, there] = beside(a[:, :BLK], b[:, :BLK])
         dv_ref[:, there] = beside(a[:, BLK:], b[:, BLK:])
-    for copy in dq_copies:
-        copy.wait_recv()
-    unfold(dq_in, dq_ref)
     for copy in all_copies:
         copy.wait_recv()
-    for i in range(dps):
-        wg_ref[i % 2 * (share // 2):(i % 2 + 1) * (share // 2),
-               i // 2 * lanes:(i // 2 + 1) * lanes] = all_in[i].astype(F32)
+    all_copies.append(push(all_in.at[core], all_in.at[core], all_sems, nz - 1, mate))
+    all_copies[-1].wait_recv()
+    for c in range(2):
+        for i in range(nz):
+            wg_ref[c * (share // 2):(c + 1) * (share // 2), i * lanes:(i + 1) * lanes] = (
+                all_in[c, i].astype(F32))
     for copy in (first + second + across + qk_copies + v_copies + b_copies + o_copies
-                 + mate_copies + line + cross + z_copies + dkv_copies + dq_copies + all_copies):
+                 + mate_copies + line_a + line_b + cross + z_copies + dkv_copies + dq_copies
+                 + all_copies):
         copy.wait_send()
 
 
@@ -493,7 +518,7 @@
         in_specs=[smem, smem, vmem, vmem, vmem] + [hbm] * 5,
         out_specs=(vmem,) * 5,
         scratch_shapes=[
-            big, big, big, big,
+            big, big, big, big, pltpu.VMEM((depth, nodes_dev), BF16),
             pltpu.VMEM((SIDE, SIDE, share, depth), BF16),
             big,
             pltpu.VMEM((nblk, nblk), jnp.int32), pltpu.SMEM((nblk, nblk), jnp.int32),
@@ -503,6 +528,7 @@
             pltpu.VMEM((listed * BLK, 256), F32),
             pltpu.VMEM((nblk // 4, listed * BLK, 256), BF16),
             pltpu.VMEM((BLK, nodes), BF16),
+            pltpu.VMEM((nodes, 128), BF16),
             pltpu.VMEM((nblk * listed + 1, BLK, 128), BF16),
             pltpu.VMEM((nodes, 256), BF16),
             folded, per_head, folded, folded, per_head, folded,
@@ -514,11 +540,11 @@
             pltpu.VMEM((2, side, rows, depth), BF16),
             pltpu.VMEM((nz, share // 2, depth // nz), BF16),
             pltpu.VMEM((few, share // 2, depth // nz), BF16),
-            pltpu.VMEM((dps, share // 2, depth // nz), BF16),
+            pltpu.VMEM((2, nz, share // 2, depth // nz), BF16),
             pltpu.SemaphoreType.DMA((5,)), pltpu.SemaphoreType.DMA,
             dma(2, side), dma(2, side), dma(4, side), dma(seq - 1), dma(seq - 1), dma(seq - 1),
-            dma(seq - 1), dma(seq - 1), dma(seq - 1), dma(SIDE), dma(2, side), dma(2, side),
-            dma(few), dma(dps - 1),
+            dma(seq - 1), dma(seq - 1), dma(seq - 1), dma(SIDE), dma(SIDE + 1, side), dma(2, side),
+            dma(few), dma(nz),
         ],
         compiler_params=pltpu.CompilerParams(
             collective_id=0, has_side_effects=True, vmem_limit_bytes=62 * 1024 * 1024),
@@ -527,13 +553,20 @@
 
 
 def finish_kernel(*refs):
-    copies = [
-        pltpu.make_async_copy(src, dst, refs[-1].at[i])
-        for i, (src, dst) in enumerate(zip(refs[:5], refs[5:10]))]
-    for copy in copies:
-        copy.start()
-    for copy in copies:
-        copy.wait()
+    arrays, outs, held, (load_sem, store_sem) = refs[:5], refs[5:10], refs[10:15], refs[15:]
+    loads = [
+        pltpu.make_async_copy(src, dst, load_sem.at[i])
+        for i, (src, dst) in enumerate(zip(arrays, held))]
+    stores = [
+        pltpu.make_async_copy(src, dst, store_sem.at[i])
+        for i, (src, dst) in enumerate(zip(held, outs))]
+    for load in loads:
+        load.start()
+    for load, store in zip(loads, stores):
+        load.wait()
+        store.start()
+    for store in stores:
+        store.wait()
 
 
 def finish(arrays):
@@ -543,7 +576,9 @@
         out_shape=tuple(jax.ShapeDtypeStruct(a.shape, a.dtype) for a in arrays),
         in_specs=[hbm] * 5,
         out_specs=(hbm,) * 5,
-        scratch_shapes=[pltpu.SemaphoreType.DMA((5,))],
+        scratch_shapes=[pltpu.VMEM(a.shape, a.dtype) for a in arrays]
+        + [pltpu.SemaphoreType.DMA((5,)), pltpu.SemaphoreType.DMA((5,))],
+        compiler_params=pltpu.CompilerParams(vmem_limit_bytes=62 * 1024 * 1024),
         name="finish",
     )(*arrays)
 

time: 136 us -> 88.7 us (0.65)
  Pallas kernels: 134 us -> 87.8 us
    pallas_call x1, Pallas kernels: 40.9 us -> 2.09 us  [finish(): pl.pallas_call(finish_kernel, out_shape=tuple((jax.ShapeDtypeStruct(a.sha...]
    pallas_call x1, Pallas kernels: 93.4 us -> 85.7 us  [fused(): pl.pallas_call(fused_kernel, out_shape=(flat, flat, flat, flat, jax.Shape...]
where the time goes in v3:
time: 88.7 us; the launch traced here: 88.6 us
  Pallas kernels  87.8 us (99%)
    pallas_call x1, Pallas kernels, fused(): pl.pallas_call(fused_kernel, out_shape=(flat, flat, flat, flat, jax.Shape...  85.7 us
    pallas_call x1, Pallas kernels, finish(): pl.pallas_call(finish_kernel, out_shape=tuple((jax.ShapeDtypeStruct(a.sha...  2.09 us

profile of v3, /device:TPU:1, one launch (start us, length us, event | category | flops | bytes accessed | tf_op | source)
XLA Modules:
  0.0 88.6 jit_solution(2923693634316013544)
XLA Ops:
  0.6 85.7 %layer.1 = (bf16[128,1024]{1,0:T(8,128)(2,1)}, bf16[128,1024]{1,0:T(8,128)(2,1)}, bf16[128,1024]{1,0:T(8,128)(2,1)}, bf16[128,1024]{1,0:T(8,128)(2,1)}, f32[64,1024]{1,0:T(8,128)}) custom-call(s32[16,32]{1,0:T(8,128)} %bitcast.20, s32[32]{0:T(128)} %bitcast.23, s32[16,32]{1,0:T(8,128)} %bitcast.21, s32[1,32]{1,0:T(1,128)} %count_vec.1, s32[16,128]{1,0:T(8,128)} %bitcast.22, ...), custom_call_target="tpu_custom_call" | custom-call | tf_op jit(solution)/shard_map/layer/pallas_call | solution.py:515
  86.3 2.1 %finish.1 = (bf16[128,1024]{1,0:T(8,128)(2,1)}, bf16[128,1024]{1,0:T(8,128)(2,1)}, bf16[128,1024]{1,0:T(8,128)(2,1)}, bf16[128,1024]{1,0:T(8,128)(2,1)}, f32[64,1024]{1,0:T(8,128)}) custom-call(bf16[128,1024]{1,0:T(8,128)(2,1)} %get-tuple-element.15.refs_0_, bf16[128,1024]{1,0:T(8,128)(2,1)} %get-tuple-element.16.refs_1_, ...), custom_call_target="tpu_custom_call" | custom-call | tf_op jit(solution)/shard_map/finish/pallas_call | solution.py:574

commit v4 on v3

--- a/solution.py
+++ b/solution.py
@@ -10,7 +10,7 @@
 STEPS = (
     (2, 2), (3, 2), (2, 3), (1, 2), (2, 1), (2, 0), (0, 2), (3, 1), (1, 3), (3, 3), (1, 1),
     (3, 0), (1, 0), (0, 3), (0, 1))
-TILE = 512
+TILE = 1024
 BLK = 64
 F32 = jnp.float32
 BF16 = jnp.bfloat16
@@ -39,7 +39,7 @@
     q_ref, k_ref, v_ref, g_ref, gt_ref, wt_ref, up_ref, slots_vec, slots_ref,
     qk_out, v_out, b_out, x_ref, v_in, b_in,
     pick_ref, unpick_ref, qq_ref, kk_ref, vv_ref, bb_ref, kt_ref, vt_ref, bt_ref,
-    score_ref, soft_ref, ot_ref, on_ref, term_ref, grads_ref,
+    score_ref, inv_ref, soft_ref, ot_ref, on_ref, term_ref, grads_ref,
     o_out, dkv_out, dq_out, o_in, dkv_in, dq_in,
     attn_ref, part_ref, mate_out, mate_in, sum_ref, half_ref, line_in, cross_out, cross_in,
     z_out, z_in, all_in,
@@ -255,43 +255,60 @@
 
     lane = lax.broadcasted_iota(jnp.int32, (1, 256), 1)
 
-    def forward(i, carry):
-        weights = diagonal(qq_ref, i)
-        live = jnp.where(
+    def live_of(i):
+        return jnp.where(
             lane < 2 * BLK,
             jnp.where(lane < BLK, count_ref[4 * i], count_ref[4 * i + 1]),
             jnp.where(lane < 3 * BLK, count_ref[4 * i + 2], count_ref[4 * i + 3]))
-        peak = jnp.full((8, 256), -jnp.inf, F32)
-        for c in range(chunks):
-            score = lax.dot_general(
-                natural(kk_ref, i, c), weights, TRANS_B, preferred_element_type=F32)
-            for k in range(4):
-                m = 4 * c + k
-                part = jnp.where(m < live, score[k * BLK:(k + 1) * BLK], -jnp.inf)
-                score_ref[m * BLK:(m + 1) * BLK, :] = part
-                peak = jnp.maximum(peak, jnp.max(part.reshape(8, 8, 256), axis=0))
+
+    def scores(i, c, weights, live, held, peak):
+        score = lax.dot_general(
+            natural(kk_ref, i, c), weights, TRANS_B, preferred_element_type=F32)
+        for k in range(4):
+            m = 4 * c + k
+            part = jnp.where(m < live, score[k * BLK:(k + 1) * BLK], -jnp.inf)
+            score_ref[held, m * BLK:(m + 1) * BLK, :] = part
+            peak = jnp.maximum(peak, jnp.max(part.reshape(8, 8, 256), axis=0))
+        return peak
+
+    no_peak = jnp.full((8, 256), -jnp.inf, F32)
+
+    def forward_step(i, held, peak):
+        after = jnp.minimum(i + 1, quads - 1)
+        weights, live = diagonal(qq_ref, after), live_of(after)
         peak = jnp.max(peak, axis=0, keepdims=True)
         total = jnp.zeros((8, 256), F32)
+        back = jnp.zeros((256, 256), F32)
+        next_peak = no_peak
         for c in range(chunks):
+            next_peak = scores(after, c, weights, live, 1 - held, next_peak)
             here = slice(c * 256, (c + 1) * 256)
-            terms = jnp.exp(score_ref[here, :] - peak)
-            score_ref[here, :] = terms
+            terms = jnp.exp(score_ref[held, here, :] - peak)
             total = total + jnp.sum(terms.reshape(32, 8, 256), axis=0)
+            terms = terms.astype(BF16)
+            soft_ref[i, here, :] = terms
+            back = back + jnp.dot(across_keys(vt_ref, i, c), terms, preferred_element_type=F32)
         inv = 1.0 / jnp.sum(total, axis=0, keepdims=True)
-        back = jnp.zeros((256, 256), F32)
-        for c in range(chunks):
-            here = slice(c * 256, (c + 1) * 256)
-            soft = (score_ref[here, :] * inv).astype(BF16)
-            soft_ref[i, here, :] = soft
-            back = back + jnp.dot(across_keys(vt_ref, i, c), soft, preferred_element_type=F32)
         there = pl.ds(pl.multiple_of(i * 256, 256), 256)
-        out = diagonal_of(back)
+        inv_ref[:, there] = inv
+        out = diagonal_of(back) * inv
         ot_ref[:, there] = out.astype(BF16)
         out = jnp.transpose(out).astype(BF16)
         on_ref[there, :] = beside(out, jnp.zeros_like(out))
-        return carry
-
-    lax.fori_loop(0, quads, forward, 0)
+        return next_peak
+
+    def forward(i, peak):
+        peak = forward_step(2 * i, 0, peak)
+        return forward_step(2 * i + 1, 1, peak)
+
+    def first_scores():
+        peak = no_peak
+        weights, live = diagonal(qq_ref, 0), live_of(0)
+        for c in range(chunks):
+            peak = scores(0, c, weights, live, 0, peak)
+        return peak
+
+    lax.fori_loop(0, quads // 2, forward, first_scores())
 
     def fold_rows(tile):
         return beside(tile[:half_nodes, :BLK], tile[half_nodes:, :BLK])
@@ -343,13 +360,20 @@
             pair_weights.append(above(
                 beside(jnp.where(low, zero, b1), zero), beside(zero, jnp.where(low, zero, b2)),
                 beside(jnp.where(low, q1, zero), zero), beside(zero, jnp.where(low, q2, zero))))
+        inv = inv_ref[:, there]
+
+        def grad_soft(c):
+            return lax.dot_general(
+                natural(vv_ref, i, c), weights, TRANS_B, preferred_element_type=F32)
+
         back = jnp.zeros((256, 256), F32)
+        grad = grad_soft(0)
         for c in range(chunks):
             here = slice(c * 256, (c + 1) * 256)
-            grad = lax.dot_general(
-                natural(vv_ref, i, c), weights, TRANS_B, preferred_element_type=F32)
-            soft = soft_ref[i, here, :]
-            grad = (soft.astype(F32) * (grad - delta)).astype(BF16)
+            ahead = grad_soft(c + 1) if c + 1 < chunks else None
+            soft = soft_ref[i, here, :].astype(F32) * inv
+            grad = (soft * (grad - delta)).astype(BF16)
+            soft = soft.astype(BF16)
             for j in range(2):
                 lanes = slice(128 * j, 128 * (j + 1))
                 terms = jnp.dot(
@@ -361,11 +385,15 @@
                     term_ref[slot] = terms[k * BLK:(k + 1) * BLK, :128]
                     term_ref[slot + listed] = terms[k * BLK:(k + 1) * BLK, 128:]
             back = back + jnp.dot(across_keys(kt_ref, i, c), grad, preferred_element_type=F32)
+            grad = ahead
         grad_q = jnp.transpose(diagonal_of(back) * 0.125).astype(BF16)
         grads_ref[there, 128:] = beside(grad_q, jnp.zeros_like(grad_q))
         return carry
 
-    lax.fori_loop(0, 4, backward, 0)
+    def backward_pair(i, carry):
+        return backward(2 * i + 1, backward(2 * i, carry))
+
+    lax.fori_loop(0, 2, backward_pair, 0)
 
     for copy in o_copies:
         copy.wait_recv()
@@ -383,7 +411,7 @@
         sum_ref[at] = part_ref[:, keep, :]
         mate_copies.append(push(mate_out.at[at], mate_in.at[at], mate_sems, c, mate))
 
-    lax.fori_loop(4, 5, backward, 0)
+    lax.fori_loop(2, 3, backward_pair, 0)
 
     line_a, line_b = [], []
     for c, at in enumerate(order_y):
@@ -403,7 +431,7 @@
         attn_ref[...], wt_ref[...].reshape(depth, depth), TRANS_B,
         preferred_element_type=F32).astype(BF16)
 
-    lax.fori_loop(5, quads, backward, 0)
+    lax.fori_loop(3, quads // 2, backward_pair, 0)
 
     back_to_nodes(grads_ref, slice(128, 256), dq_out, fold_rows)
     dq_in[me] = dq_out[me]
@@ -411,9 +439,10 @@
         push(dq_out.at[p], dq_in.at[me], dq_sems, i, (dp, p)) for i, p in enumerate(peers)]
 
     def gather_terms(c, carry):
-        total = term_ref[slots_ref[c, 0]].astype(F32)
-        for r in range(1, nblk):
-            total = total + term_ref[slots_ref[c, r]].astype(F32)
+        total = jnp.zeros((BLK, 128), F32)
+        for r in range(0, nblk, 2):
+            pair = term_ref[slots_ref[c, r]] + term_ref[slots_ref[c, r + 1]]
+            total = total + pair.astype(F32)
         grads_ref[pl.ds(pl.multiple_of(c * BLK, BLK), BLK), :128] = total.astype(BF16)
         return carry
 
@@ -525,7 +554,7 @@
             per_head, folded, folded, pltpu.VMEM((nodes, 256), BF16), folded, folded,
             pick, pick, blocks, blocks, blocks, blocks, turned, turned,
             pltpu.VMEM((BLK, nodes), F32),
-            pltpu.VMEM((listed * BLK, 256), F32),
+            pltpu.VMEM((2, listed * BLK, 256), F32), pltpu.VMEM((1, nodes), F32),
             pltpu.VMEM((nblk // 4, listed * BLK, 256), BF16),
             pltpu.VMEM((BLK, nodes), BF16),
             pltpu.VMEM((nodes, 128), BF16),

time: 88.7 us -> 80.7 us (0.910)
  Pallas kernels: 87.8 us -> 79.7 us
    pallas_call x1, Pallas kernels: 85.7 us -> 77.6 us  [fused(): pl.pallas_call(fused_kernel, out_shape=(flat, flat, flat, flat, jax.Shape...]
where the time goes in v4:
time: 80.7 us; the launch traced here: 80.5 us
  Pallas kernels  79.7 us (99%)
  between operations  0.82 us (1%)
    pallas_call x1, Pallas kernels, fused(): pl.pallas_call(fused_kernel, out_shape=(flat, flat, flat, flat, jax.Shape...  77.6 us
    pallas_call x1, Pallas kernels, finish(): pl.pallas_call(finish_kernel, out_shape=tuple((jax.ShapeDtypeStruct(a.sha...  2.09 us

profile of v4, /device:TPU:1, one launch (start us, length us, event | category | flops | bytes accessed | tf_op | source)
XLA Modules:
  0.0 80.5 jit_solution(5671884607376272538)
XLA Ops:
  0.6 77.6 %layer.1 = (bf16[128,1024]{1,0:T(8,128)(2,1)}, bf16[128,1024]{1,0:T(8,128)(2,1)}, bf16[128,1024]{1,0:T(8,128)(2,1)}, bf16[128,1024]{1,0:T(8,128)(2,1)}, f32[64,1024]{1,0:T(8,128)}) custom-call(s32[16,32]{1,0:T(8,128)} %bitcast.20, s32[32]{0:T(128)} %bitcast.23, s32[16,32]{1,0:T(8,128)} %bitcast.21, s32[1,32]{1,0:T(1,128)} %count_vec.1, s32[16,128]{1,0:T(8,128)} %bitcast.22, ...), custom_call_target="tpu_custom_call" | custom-call | tf_op jit(solution)/shard_map/layer/pallas_call | solution.py:544
  78.3 2.1 %finish.1 = (bf16[128,1024]{1,0:T(8,128)(2,1)}, bf16[128,1024]{1,0:T(8,128)(2,1)}, bf16[128,1024]{1,0:T(8,128)(2,1)}, bf16[128,1024]{1,0:T(8,128)(2,1)}, f32[64,1024]{1,0:T(8,128)}) custom-call(bf16[128,1024]{1,0:T(8,128)(2,1)} %get-tuple-element.15.refs_0_, bf16[128,1024]{1,0:T(8,128)(2,1)} %get-tuple-element.16.refs_1_, ...), custom_call_target="tpu_custom_call" | custom-call | tf_op jit(solution)/shard_map/finish/pallas_call | solution.py:603

commit v5 on v4

--- a/solution.py
+++ b/solution.py
@@ -35,17 +35,20 @@
 
 def fused_kernel(
     cols_ref, count_ref, cols_vec, count_vec, order_ref, q_hbm, k_hbm, v_hbm, g_hbm, w_hbm,
-    layer_ref, dq_ref, dk_ref, dv_ref, wg_ref,
-    q_ref, k_ref, v_ref, g_ref, gt_ref, wt_ref, up_ref, slots_vec, slots_ref,
-    qk_out, v_out, b_out, x_ref, v_in, b_in,
-    pick_ref, unpick_ref, qq_ref, kk_ref, vv_ref, bb_ref, kt_ref, vt_ref, bt_ref,
-    score_ref, inv_ref, soft_ref, ot_ref, on_ref, term_ref, grads_ref,
-    o_out, dkv_out, dq_out, o_in, dkv_in, dq_in,
-    attn_ref, part_ref, mate_out, mate_in, sum_ref, half_ref, line_in, cross_out, cross_in,
-    z_out, z_in, all_in,
-    in_sem, slot_sem, w1_sems, w2_sems, core_sems, qk_sems, v_sems, b_sems,
-    o_sems, dkv_sems, dq_sems, mate_sems, line_sems, cross_sems, z_sems, all_sems,
+    *rest,
 ):
+    outs, (layer_ref, dq_ref, dk_ref, dv_ref, wg_ref) = rest[:5], rest[5:10]
+    (
+        q_ref, k_ref, v_ref, g_ref, gt_ref, wt_ref, up_ref, slots_vec, slots_ref,
+        qk_out, v_out, b_out, x_ref, v_in, b_in,
+        pick_ref, unpick_ref, qq_ref, kk_ref, vv_ref, bb_ref, kt_ref, vt_ref, bt_ref,
+        score_ref, inv_ref, soft_ref, ot_ref, on_ref, term_ref, grads_ref,
+        o_out, dkv_out, dq_out, o_in, dkv_in, dq_in,
+        attn_ref, part_ref, mate_out, mate_in, sum_ref, half_ref, line_in, cross_out, cross_in,
+        z_out, z_in, all_in,
+        in_sem, out_sem, slot_sem, w1_sems, w2_sems, core_sems, qk_sems, v_sems, b_sems,
+        o_sems, dkv_sems, dq_sems, mate_sems, line_sems, cross_sems, z_sems, all_sems,
+    ) = rest[10:]
     dp, me = lax.axis_index("dp"), lax.axis_index("seq")
     seq, half_nodes, _ = v_out.shape
     nz = all_in.shape[1]
@@ -78,6 +81,14 @@
             (g_hbm, g_ref)))]
     for load in loads:
         load.start()
+    results = (layer_ref, dq_ref, dk_ref, dv_ref, wg_ref)
+    stores = [
+        pltpu.make_async_copy(src, dst, out_sem.at[i])
+        for i, (src, dst) in enumerate(zip(results, outs))]
+
+    def store(i):
+        stores[i].start()
+
     barrier = pltpu.get_barrier_semaphore()
     greeted = [(dp, p) for p in peers] + [(2 * p + core, me) for p in z_peers] + [mate]
     for device in greeted:
@@ -88,14 +99,6 @@
     start_a = pl.multiple_of(core * 2 * rows, 2 * rows)
     half_a = pl.ds(start_a, rows)
     half_b = pl.ds(pl.multiple_of(start_a + rows, rows), rows)
-    loads[0].wait()
-    first, second, across = [], [], []
-    for i in range(SIDE - 1):
-        piece = wt_ref.at[y, x, half_a]
-        first.append(push(piece, piece, w1_sems, (0, i), x_peers[i]))
-        piece = wt_ref.at[y, x, half_b]
-        first.append(push(piece, piece, w1_sems, (1, i), y_peers[i]))
-
     loads[1].wait()
     loads[2].wait()
     for j in range(seq // 2):
@@ -128,6 +131,14 @@
     v_copies = [
         push(v_out.at[p], v_in.at[me], v_sems, i, (dp, p)) for i, p in enumerate(peers)]
 
+    loads[0].wait()
+    first, second, across = [], [], []
+    for i in range(SIDE - 1):
+        piece = wt_ref.at[y, x, half_a]
+        first.append(push(piece, piece, w1_sems, (0, i), x_peers[i]))
+        piece = wt_ref.at[y, x, half_b]
+        first.append(push(piece, piece, w1_sems, (1, i), y_peers[i]))
+
     order = order_ref[...]
     order_col = jnp.transpose(
         above(order.astype(F32), jnp.zeros((128 - order.shape[0], 128), F32))).astype(jnp.int32)
@@ -136,20 +147,7 @@
         pick_ref[128 * i:128 * (i + 1), :] = (
             lane_node == order_col[:, i:i + 1]).astype(F32).astype(BF16)
 
-    for copy in first:
-        copy.wait_recv()
     loads[4].wait()
-    for i in range(SIDE - 1):
-        piece = wt_ref.at[y, :, half_a]
-        second.append(push(piece, piece, w2_sems, (0, i), y_peers[i]))
-        piece = wt_ref.at[:, x, half_b]
-        second.append(push(piece, piece, w2_sems, (1, i), x_peers[i]))
-    for i in range(SIDE - 1):
-        piece = wt_ref.at[y, xs[i], half_a]
-        across.append(push(piece, piece, core_sems, (0, i), mate))
-        piece = wt_ref.at[ys[i], x, half_b]
-        across.append(push(piece, piece, core_sems, (1, i), mate))
-
     for i in range(depth // 128):
         gt_ref[128 * i:128 * (i + 1), :] = jnp.transpose(g_ref[:, 128 * i:128 * (i + 1)])
     order_row = jnp.concatenate([order[i:i + 1, :] for i in range(nodes // 128)], axis=1)
@@ -170,6 +168,19 @@
 
     for copy in qk_copies + v_copies:
         copy.wait_recv()
+    for copy in first:
+        copy.wait_recv()
+    for i in range(SIDE - 1):
+        piece = wt_ref.at[y, :, half_a]
+        second.append(push(piece, piece, w2_sems, (0, i), y_peers[i]))
+        piece = wt_ref.at[:, x, half_b]
+        second.append(push(piece, piece, w2_sems, (1, i), x_peers[i]))
+    for i in range(SIDE - 1):
+        piece = wt_ref.at[y, xs[i], half_a]
+        across.append(push(piece, piece, core_sems, (0, i), mate))
+        piece = wt_ref.at[ys[i], x, half_b]
+        across.append(push(piece, piece, core_sems, (1, i), mate))
+
     slot_copy.wait()
     empty = jnp.zeros((half_nodes, BLK), BF16)
     for s in range(seq):
@@ -205,23 +216,6 @@
         return carry
 
     lax.fori_loop(0, nodes // TILE, into_cluster, 0)
-
-    for i in range(SIDE - 1):
-        back = SIDE - 1 - i
-        second[2 * i].wait_recv()
-        piece = wt_ref.at[lax.rem(y + back, SIDE), :, half_a]
-        across.append(push(piece, piece, core_sems, (2, i), mate))
-        second[2 * i + 1].wait_recv()
-        piece = wt_ref.at[:, lax.rem(x + back, SIDE), half_b]
-        across.append(push(piece, piece, core_sems, (3, i), mate))
-    for copy in across:
-        copy.wait_recv()
-    up_ref[...] = jnp.dot(
-        g_ref[...], wt_ref[...].reshape(depth, depth), preferred_element_type=F32).astype(BF16)
-    fold(up_ref, b_out)
-    b_in[me] = b_out[me]
-    b_copies = [
-        push(b_out.at[p], b_in.at[me], b_sems, i, (dp, p)) for i, p in enumerate(peers)]
 
     def diagonal(ref, i):
         blocks = []
@@ -310,6 +304,14 @@
 
     lax.fori_loop(0, quads // 2, forward, first_scores())
 
+    for i in range(SIDE - 1):
+        back = SIDE - 1 - i
+        second[2 * i].wait_recv()
+        piece = wt_ref.at[lax.rem(y + back, SIDE), :, half_a]
+        across.append(push(piece, piece, core_sems, (2, i), mate))
+        second[2 * i + 1].wait_recv()
+        piece = wt_ref.at[:, lax.rem(x + back, SIDE), half_b]
+        across.append(push(piece, piece, core_sems, (3, i), mate))
     def fold_rows(tile):
         return beside(tile[:half_nodes, :BLK], tile[half_nodes:, :BLK])
 
@@ -329,6 +331,51 @@
     o_copies = [
         push(o_out.at[p], o_in.at[me], o_sems, i, (dp, p)) for i, p in enumerate(peers)]
 
+    for copy in across:
+        copy.wait_recv()
+    up_ref[...] = jnp.dot(
+        g_ref[...], wt_ref[...].reshape(depth, depth), preferred_element_type=F32).astype(BF16)
+    fold(up_ref, b_out)
+    b_in[me] = b_out[me]
+    b_copies = [
+        push(b_out.at[p], b_in.at[me], b_sems, i, (dp, p)) for i, p in enumerate(peers)]
+
+    for copy in o_copies:
+        copy.wait_recv()
+    unfold(o_in, attn_ref)
+    keep = pl.ds(pl.multiple_of(core * (share // 2), share // 2), share // 2)
+    give = pl.ds(pl.multiple_of((1 - core) * (share // 2), share // 2), share // 2)
+    order_y = ys + [y]
+    mate_copies = []
+    for c, at in enumerate(order_y):
+        there = pl.ds(pl.multiple_of(at * (SIDE * share), SIDE * share), SIDE * share)
+        part_ref[...] = jnp.dot(
+            gt_ref[there, :], attn_ref[...], preferred_element_type=F32).reshape(
+                SIDE, share, depth)
+        mate_out[at] = part_ref[:, give, :].astype(BF16)
+        sum_ref[at] = part_ref[:, keep, :]
+        mate_copies.append(push(mate_out.at[at], mate_in.at[at], mate_sems, c, mate))
+
+    layer_ref[...] = lax.dot_general(
+        attn_ref[...], wt_ref[...].reshape(depth, depth), TRANS_B,
+        preferred_element_type=F32).astype(BF16)
+
+    store(0)
+
+    line_a, line_b = [], []
+    for c, at in enumerate(order_y):
+        mate_copies[c].wait_recv()
+        total = sum_ref[at] + mate_in[at].astype(F32)
+        sum_ref[at] = total
+        half_ref[at] = total.astype(BF16)
+        for i in range(SIDE - 1):
+            line_a.append(push(
+                half_ref.at[at, xs[i], pl.ds(0, rows)], line_in.at[0, i, at], line_sems, (c, i),
+                x_peers[i]))
+        if c < SIDE - 1:
+            line_b.append(push(
+                half_ref.at[at, :, pl.ds(rows, rows)], line_in.at[1, c], line_sems, (SIDE, c),
+                y_peers[c]))
     for copy in b_copies:
         copy.wait_recv()
     for s in range(seq):
@@ -393,60 +440,7 @@
     def backward_pair(i, carry):
         return backward(2 * i + 1, backward(2 * i, carry))
 
-    lax.fori_loop(0, 2, backward_pair, 0)
-
-    for copy in o_copies:
-        copy.wait_recv()
-    unfold(o_in, attn_ref)
-    keep = pl.ds(pl.multiple_of(core * (share // 2), share // 2), share // 2)
-    give = pl.ds(pl.multiple_of((1 - core) * (share // 2), share // 2), share // 2)
-    order_y = ys + [y]
-    mate_copies = []
-    for c, at in enumerate(order_y):
-        there = pl.ds(pl.multiple_of(at * (SIDE * share), SIDE * share), SIDE * share)
-        part_ref[...] = jnp.dot(
-            gt_ref[there, :], attn_ref[...], preferred_element_type=F32).reshape(
-                SIDE, share, depth)
-        mate_out[at] = part_ref[:, give, :].astype(BF16)
-        sum_ref[at] = part_ref[:, keep, :]
-        mate_copies.append(push(mate_out.at[at], mate_in.at[at], mate_sems, c, mate))
-
-    lax.fori_loop(2, 3, backward_pair, 0)
-
-    line_a, line_b = [], []
-    for c, at in enumerate(order_y):
-        mate_copies[c].wait_recv()
-        total = sum_ref[at] + mate_in[at].astype(F32)
-        sum_ref[at] = total
-        half_ref[at] = total.astype(BF16)
-        for i in range(SIDE - 1):
-            line_a.append(push(
-                half_ref.at[at, xs[i], pl.ds(0, rows)], line_in.at[0, i, at], line_sems, (c, i),
-                x_peers[i]))
-        if c < SIDE - 1:
-            line_b.append(push(
-                half_ref.at[at, :, pl.ds(rows, rows)], line_in.at[1, c], line_sems, (SIDE, c),
-                y_peers[c]))
-    layer_ref[...] = lax.dot_general(
-        attn_ref[...], wt_ref[...].reshape(depth, depth), TRANS_B,
-        preferred_element_type=F32).astype(BF16)
-
-    lax.fori_loop(3, quads // 2, backward_pair, 0)
-
-    back_to_nodes(grads_ref, slice(128, 256), dq_out, fold_rows)
-    dq_in[me] = dq_out[me]
-    dq_copies = [
-        push(dq_out.at[p], dq_in.at[me], dq_sems, i, (dp, p)) for i, p in enumerate(peers)]
-
-    def gather_terms(c, carry):
-        total = jnp.zeros((BLK, 128), F32)
-        for r in range(0, nblk, 2):
-            pair = term_ref[slots_ref[c, r]] + term_ref[slots_ref[c, r + 1]]
-            total = total + pair.astype(F32)
-        grads_ref[pl.ds(pl.multiple_of(c * BLK, BLK), BLK), :128] = total.astype(BF16)
-        return carry
-
-    lax.fori_loop(0, nblk, gather_terms, 0)
+    lax.fori_loop(0, quads // 2, backward_pair, 0)
 
     for copy in line_a + line_b:
         copy.wait_recv()
@@ -464,6 +458,16 @@
         cross.append(push(
             cross_out.at[1, xs[i]], cross_in.at[1, i], cross_sems, (1, i), x_peers[i]))
 
+    def gather_terms(c, carry):
+        total = jnp.zeros((BLK, 128), F32)
+        for r in range(0, nblk, 2):
+            pair = term_ref[slots_ref[c, r]] + term_ref[slots_ref[c, r + 1]]
+            total = total + pair.astype(F32)
+        grads_ref[pl.ds(pl.multiple_of(c * BLK, BLK), BLK), :128] = total.astype(BF16)
+        return carry
+
+    lax.fori_loop(0, nblk, gather_terms, 0)
+
     back_to_nodes(grads_ref, slice(0, 128), dkv_out, lambda tile: tile)
     dkv_in[me] = dkv_out[me]
     dkv_copies = [
@@ -483,9 +487,11 @@
     z_copies = [
         push(z_out.at[p], z_in.at[i], z_sems, i, (2 * p + core, me))
         for i, p in enumerate(z_peers)]
-    for copy in dq_copies:
-        copy.wait_recv()
-    unfold(dq_in, dq_ref)
+    back_to_nodes(grads_ref, slice(128, 256), dq_out, fold_rows)
+    dq_in[me] = dq_out[me]
+    dq_copies = [
+        push(dq_out.at[p], dq_in.at[me], dq_sems, i, (dp, p)) for i, p in enumerate(peers)]
+
     for copy in z_copies:
         copy.wait_recv()
     mine = z_out[z].astype(F32)
@@ -503,6 +509,12 @@
         a, b = dkv_in[2 * j], dkv_in[2 * j + 1]
         dk_ref[:, there] = beside(a[:, :BLK], b[:, :BLK])
         dv_ref[:, there] = beside(a[:, BLK:], b[:, BLK:])
+    store(2)
+    store(3)
+    for copy in dq_copies:
+        copy.wait_recv()
+    unfold(dq_in, dq_ref)
+    store(1)
     for copy in all_copies:
         copy.wait_recv()
     all_copies.append(push(all_in.at[core], all_in.at[core], all_sems, nz - 1, mate))
@@ -511,10 +523,13 @@
         for i in range(nz):
             wg_ref[c * (share // 2):(c + 1) * (share // 2), i * lanes:(i + 1) * lanes] = (
                 all_in[c, i].astype(F32))
+    store(4)
     for copy in (first + second + across + qk_copies + v_copies + b_copies + o_copies
                  + mate_copies + line_a + line_b + cross + z_copies + dkv_copies + dq_copies
                  + all_copies):
         copy.wait_send()
+    for copy in stores:
+        copy.wait()
 
 
 def fused(q, k, v, g, wt, order, cols, count, seq, dps):
@@ -545,8 +560,9 @@
         fused_kernel,
         out_shape=(flat, flat, flat, flat, jax.ShapeDtypeStruct((share, depth), F32)),
         in_specs=[smem, smem, vmem, vmem, vmem] + [hbm] * 5,
-        out_specs=(vmem,) * 5,
+        out_specs=(hbm,) * 5,
         scratch_shapes=[
+            big, big, big, big, pltpu.VMEM((share, depth), F32),
             big, big, big, big, pltpu.VMEM((depth, nodes_dev), BF16),
             pltpu.VMEM((SIDE, SIDE, share, depth), BF16),
             big,
@@ -570,7 +586,7 @@
             pltpu.VMEM((nz, share // 2, depth // nz), BF16),
             pltpu.VMEM((few, share // 2, depth // nz), BF16),
             pltpu.VMEM((2, nz, share // 2, depth // nz), BF16),
-            pltpu.SemaphoreType.DMA((5,)), pltpu.SemaphoreType.DMA,
+            pltpu.SemaphoreType.DMA((5,)), pltpu.SemaphoreType.DMA((5,)), pltpu.SemaphoreType.DMA,
             dma(2, side), dma(2, side), dma(4, side), dma(seq - 1), dma(seq - 1), dma(seq - 1),
             dma(seq - 1), dma(seq - 1), dma(seq - 1), dma(SIDE), dma(SIDE + 1, side), dma(2, side),
             dma(few), dma(nz),

time: 80.7 us -> 79.2 us (0.981)
  Pallas kernels: 79.7 us -> 78.2 us
    pallas_call x1, Pallas kernels: 77.6 us -> 76.2 us  [fused(): pl.pallas_call(fused_kernel, out_shape=(flat, flat, flat, flat, jax.Shape...]
where the time goes in v5:
time: 79.2 us; the launch traced here: 79 us
  Pallas kernels  78.2 us (99%)
  between operations  0.8 us (1%)
    pallas_call x1, Pallas kernels, fused(): pl.pallas_call(fused_kernel, out_shape=(flat, flat, flat, flat, jax.Shape...  76.2 us
    pallas_call x1, Pallas kernels, finish(): pl.pallas_call(finish_kernel, out_shape=tuple((jax.ShapeDtypeStruct(a.sha...  2.09 us

profile of v5, /device:TPU:1, one launch (start us, length us, event | category | flops | bytes accessed | tf_op | source)
XLA Modules:
  0.0 79.0 jit_solution(14764714924832657885)
XLA Ops:
  0.6 76.2 %layer.1 = (bf16[128,1024]{1,0:T(8,128)(2,1)}, bf16[128,1024]{1,0:T(8,128)(2,1)}, bf16[128,1024]{1,0:T(8,128)(2,1)}, bf16[128,1024]{1,0:T(8,128)(2,1)}, f32[64,1024]{1,0:T(8,128)}) custom-call(s32[16,32]{1,0:T(8,128)} %bitcast.20, s32[32]{0:T(128)} %bitcast.23, s32[16,32]{1,0:T(8,128)} %bitcast.21, s32[1,32]{1,0:T(1,128)} %count_vec.1, s32[16,128]{1,0:T(8,128)} %bitcast.22, ...), custom_call_target="tpu_custom_call" | custom-call | tf_op jit(solution)/shard_map/layer/pallas_call | solution.py:559
  76.8 2.1 %finish.1 = (bf16[128,1024]{1,0:T(8,128)(2,1)}, bf16[128,1024]{1,0:T(8,128)(2,1)}, bf16[128,1024]{1,0:T(8,128)(2,1)}, bf16[128,1024]{1,0:T(8,128)(2,1)}, f32[64,1024]{1,0:T(8,128)}) custom-call(bf16[128,1024]{1,0:T(8,128)(2,1)} %get-tuple-element.15.refs_0_, bf16[128,1024]{1,0:T(8,128)(2,1)} %get-tuple-element.16.refs_1_, ...), custom_call_target="tpu_custom_call" | custom-call | tf_op jit(solution)/shard_map/finish/pallas_call | solution.py:619

commit v6 on v5

--- a/solution.py
+++ b/solution.py
@@ -166,7 +166,37 @@
     slot_copy.start()
     term_ref[nblk * listed] = zero
 
-    for copy in qk_copies + v_copies:
+    for copy in qk_copies:
+        copy.wait_recv()
+    slot_copy.wait()
+
+    def turned(ref, i, tile):
+        swap = pltpu.roll(tile, BLK, 1).astype(BF16)
+        tile = tile.astype(BF16)
+        ref[0, 2 * i] = jnp.where(low, tile, zero)
+        ref[1, 2 * i] = jnp.where(low, zero, swap)
+        ref[0, 2 * i + 1] = jnp.where(low, swap, zero)
+        ref[1, 2 * i + 1] = jnp.where(low, zero, tile)
+
+    def twice(ref, i, tile):
+        ref[2 * i] = tile[:BLK]
+        ref[2 * i + 1] = tile[BLK:]
+
+    def keys_into_cluster(t, carry):
+        here = pl.ds(pl.multiple_of(t * TILE, TILE), TILE)
+        tile = jnp.dot(pick_ref[here, :], x_ref[:, :128], preferred_element_type=F32)
+        for k in range(TILE // 128):
+            qk = tile[128 * k:128 * (k + 1)]
+            i = t * (TILE // 128) + k
+            kq = pltpu.roll(qk, BLK, 1)
+            twice(qq_ref, i, (jnp.where(low128, qk, kq) * 0.125).astype(BF16))
+            twice(kk_ref, i, jnp.where(low128, kq, qk).astype(BF16))
+            turned(kt_ref, i, jnp.transpose(qk)[BLK:])
+        return carry
+
+    lax.fori_loop(0, nodes // TILE, keys_into_cluster, 0)
+
+    for copy in v_copies:
         copy.wait_recv()
     for copy in first:
         copy.wait_recv()
@@ -181,41 +211,23 @@
         piece = wt_ref.at[ys[i], x, half_b]
         across.append(push(piece, piece, core_sems, (1, i), mate))
 
-    slot_copy.wait()
     empty = jnp.zeros((half_nodes, BLK), BF16)
     for s in range(seq):
         tile = v_in[s]
         x_ref[nodes_dev * s:nodes_dev * s + half_nodes, 128:] = beside(tile[:, :BLK], empty)
         x_ref[nodes_dev * s + half_nodes:nodes_dev * (s + 1), 128:] = beside(tile[:, BLK:], empty)
 
-    def turned(ref, i, tile):
-        swap = pltpu.roll(tile, BLK, 1).astype(BF16)
-        tile = tile.astype(BF16)
-        ref[0, 2 * i] = jnp.where(low, tile, zero)
-        ref[1, 2 * i] = jnp.where(low, zero, swap)
-        ref[0, 2 * i + 1] = jnp.where(low, swap, zero)
-        ref[1, 2 * i + 1] = jnp.where(low, zero, tile)
-
-    def twice(ref, i, tile):
-        ref[2 * i] = tile[:BLK]
-        ref[2 * i + 1] = tile[BLK:]
-
-    def into_cluster(t, carry):
+    def values_into_cluster(t, carry):
         here = pl.ds(pl.multiple_of(t * TILE, TILE), TILE)
-        tile = jnp.dot(pick_ref[here, :], x_ref[...], preferred_element_type=F32)
+        tile = jnp.dot(pick_ref[here, :], x_ref[:, 128:], preferred_element_type=F32)
         for k in range(TILE // 128):
-            moved = tile[128 * k:128 * (k + 1)]
+            v = tile[128 * k:128 * (k + 1)]
             i = t * (TILE // 128) + k
-            qk, v = moved[:, :128], moved[:, 128:]
-            kq = pltpu.roll(qk, BLK, 1)
-            twice(qq_ref, i, (jnp.where(low128, qk, kq) * 0.125).astype(BF16))
-            twice(kk_ref, i, jnp.where(low128, kq, qk).astype(BF16))
             twice(vv_ref, i, (v + pltpu.roll(v, BLK, 1)).astype(BF16))
-            turned(kt_ref, i, jnp.transpose(qk)[BLK:])
             turned(vt_ref, i, jnp.transpose(v)[:BLK])
         return carry
 
-    lax.fori_loop(0, nodes // TILE, into_cluster, 0)
+    lax.fori_loop(0, nodes // TILE, values_into_cluster, 0)
 
     def diagonal(ref, i):
         blocks = []
@@ -356,12 +368,6 @@
         sum_ref[at] = part_ref[:, keep, :]
         mate_copies.append(push(mate_out.at[at], mate_in.at[at], mate_sems, c, mate))
 
-    layer_ref[...] = lax.dot_general(
-        attn_ref[...], wt_ref[...].reshape(depth, depth), TRANS_B,
-        preferred_element_type=F32).astype(BF16)
-
-    store(0)
-
     line_a, line_b = [], []
     for c, at in enumerate(order_y):
         mate_copies[c].wait_recv()
@@ -376,6 +382,12 @@
             line_b.append(push(
                 half_ref.at[at, :, pl.ds(rows, rows)], line_in.at[1, c], line_sems, (SIDE, c),
                 y_peers[c]))
+    layer_ref[...] = lax.dot_general(
+        attn_ref[...], wt_ref[...].reshape(depth, depth), TRANS_B,
+        preferred_element_type=F32).astype(BF16)
+
+    store(0)
+
     for copy in b_copies:
         copy.wait_recv()
     for s in range(seq):

time: 79.2 us -> 78.7 us (level)
  no operation moved by 1% of the time
where the time goes in v6:
time: 78.7 us; the launch traced here: 78.5 us
  Pallas kernels  77.7 us (99%)
  between operations  0.8 us (1%)
    pallas_call x1, Pallas kernels, fused(): pl.pallas_call(fused_kernel, out_shape=(flat, flat, flat, flat, jax.Shape...  75.7 us
    pallas_call x1, Pallas kernels, finish(): pl.pallas_call(finish_kernel, out_shape=tuple((jax.ShapeDtypeStruct(a.sha...  2.09 us

profile of v6, /device:TPU:1, one launch (start us, length us, event | category | flops | bytes accessed | tf_op | source)
XLA Modules:
  0.0 78.5 jit_solution(11294699027721493268)
XLA Ops:
  0.6 75.7 %layer.1 = (bf16[128,1024]{1,0:T(8,128)(2,1)}, bf16[128,1024]{1,0:T(8,128)(2,1)}, bf16[128,1024]{1,0:T(8,128)(2,1)}, bf16[128,1024]{1,0:T(8,128)(2,1)}, f32[64,1024]{1,0:T(8,128)}) custom-call(s32[16,32]{1,0:T(8,128)} %bitcast.20, s32[32]{0:T(128)} %bitcast.23, s32[16,32]{1,0:T(8,128)} %bitcast.21, s32[1,32]{1,0:T(1,128)} %count_vec.1, s32[16,128]{1,0:T(8,128)} %bitcast.22, ...), custom_call_target="tpu_custom_call" | custom-call | tf_op jit(solution)/shard_map/layer/pallas_call | solution.py:571
  76.3 2.1 %finish.1 = (bf16[128,1024]{1,0:T(8,128)(2,1)}, bf16[128,1024]{1,0:T(8,128)(2,1)}, bf16[128,1024]{1,0:T(8,128)(2,1)}, bf16[128,1024]{1,0:T(8,128)(2,1)}, f32[64,1024]{1,0:T(8,128)}) custom-call(bf16[128,1024]{1,0:T(8,128)(2,1)} %get-tuple-element.15.refs_0_, bf16[128,1024]{1,0:T(8,128)(2,1)} %get-tuple-element.16.refs_1_, ...), custom_call_target="tpu_custom_call" | custom-call | tf_op jit(solution)/shard_map/finish/pallas_call | solution.py:631
